TPU v7x, 32 devices: a whole 2x2x4 slice. The times are simulated.
32 devices in a mesh: dp: 16 (over z, y, core), mp: 2 (over x).
Axes of the slice: x: 2, y: 2, z: 4, core: 2. Of those that a mesh axis runs over, the one named last changes fastest.
Arguments:
- frames_in: bfloat16 [16384, 1536], P('dp', 'mp')
- lengths: int32 [64], P('dp'), may hold values from 42 to 256, as said below
- ln_gain: float32 [1536], P('mp'), may hold values from 0.1 to 1.9
- ln_bias: float32 [1536], P('mp'), may hold values from -3 to 3
- kernel: float32 [31, 1536], P(None, 'mp'), may hold values from -1 to 1
- point_weight: bfloat16 [1536, 1536], P('dp', 'mp'), may hold values from -0.15625 to 0.15625
- target: bfloat16 [16384, 1536], P('dp')
Outputs:
- frames_grad: bfloat16 [16384, 1536], P('dp', 'mp')
- weight_grad: float32 [1536, 1536], P('dp', 'mp')
- kernel_grad: float32 [31, 1536], P(None, 'mp')
- gain_grad: float32 [1536], P('mp')
- bias_grad: float32 [1536], P('mp')
Inputs may be any that keep to these rules, and one draw needn't show every extreme that they name: `lengths`: valid frames of each utterance slot; some slot has exactly 256.
All inputs are finite; a program needn't handle non-finite values.
Results may differ from a plain program's by a relative error of at most 0.001.
Values may be sent and summed in bfloat16 or wider, within the bound.
A program may use at most 64 MiB of HBM per device.

v0:
```python
import jax
import jax.numpy as jnp
from jax import lax
from jax.sharding import PartitionSpec as P

epsilon = 1e-05


def depthwise(inputs, taps):
    half = (taps.shape[0] - 1) // 2
    return lax.conv_general_dilated(
        inputs,
        taps[:, None, :],
        (1,),
        [(half, half)],
        dimension_numbers=("NWC", "WIO", "NWC"),
        feature_group_count=inputs.shape[2],
        precision=lax.Precision.HIGHEST,
    )


def body(frames_in, lengths, ln_gain, ln_bias, kernel, point_weight, target):
    tok_rows, chan_count = frames_in.shape
    utt_count = lengths.shape[0]
    frame_count = tok_rows // utt_count
    full_width = target.shape[1]
    position = lax.broadcasted_iota(jnp.int32, (utt_count, frame_count), 1)
    valid_mask = (position < lengths[:, None]).astype(jnp.float32).reshape(tok_rows, 1)
    local_total = jnp.sum(lengths).astype(jnp.float32)
    values = frames_in.astype(jnp.float32)
    row_mean = lax.psum(jnp.sum(values, axis=1), "mp") / full_width
    centered = values - row_mean[:, None]
    row_var = lax.psum(jnp.sum(centered * centered, axis=1), "mp") / full_width
    inv_std = lax.rsqrt(row_var + epsilon)[:, None]
    normed = centered * inv_std
    masked = (normed * ln_gain + ln_bias) * valid_mask
    conv_out, conv_back = jax.vjp(
        depthwise, masked.reshape(utt_count, frame_count, chan_count), kernel
    )
    pre_act = conv_out.reshape(tok_rows, chan_count)
    gate_sig = jax.nn.sigmoid(pre_act)
    activation = (pre_act * gate_sig).astype(jnp.bfloat16)
    cotangent = target * valid_mask.astype(jnp.bfloat16)
    columns = cotangent
    act_grad = jnp.dot(
        columns,
        lax.all_gather(point_weight, "dp", axis=0, tiled=True),
        preferred_element_type=jnp.float32,
    )
    pre_grad = act_grad * gate_sig * (1.0 + pre_act * (1.0 - gate_sig))
    back_in, kernel_part = conv_back(pre_grad.reshape(utt_count, frame_count, chan_count))
    masked_grad = back_in.reshape(tok_rows, chan_count) * valid_mask
    gain_part = jnp.sum(masked_grad * normed, axis=0)
    bias_part = jnp.sum(masked_grad, axis=0)
    hat_grad = masked_grad * ln_gain
    hat_sum, hat_dot = lax.psum(
        (jnp.sum(hat_grad, axis=1), jnp.sum(hat_grad * normed, axis=1)), "mp"
    )
    norm_grad = inv_std * (
        hat_grad - hat_sum[:, None] / full_width - normed * (hat_dot[:, None] / full_width)
    )
    columns = cotangent
    term = lax.dot_general(
        columns, activation, (((0,), (0,)), ((), ())), preferred_element_type=jnp.float32
    )
    weight_grad = lax.psum_scatter(term, "dp", scatter_dimension=0, tiled=True)
    kernel_sum, gain_sum, bias_sum, frame_total = lax.psum(
        (kernel_part, gain_part, bias_part, local_total), "dp"
    )
    inverse = 1.0 / frame_total
    kernel_grad = kernel_sum * inverse
    gain_grad = gain_sum * inverse
    bias_grad = bias_sum * inverse
    weight_grad = weight_grad * inverse
    own_grad = lax.dynamic_slice_in_dim(
        cotangent, lax.axis_index("mp") * chan_count, chan_count, 1
    ).astype(jnp.float32)
    slot_total = tok_rows * lax.axis_size("dp")
    frames_grad = ((own_grad + norm_grad) * (slot_total * inverse)).astype(jnp.bfloat16)
    return (frames_grad, weight_grad, kernel_grad, gain_grad, bias_grad)


def solution(mesh):
    return jax.shard_map(
        body,
        mesh=mesh,
        in_specs=(
            P("dp", "mp"),
            P("dp"),
            P("mp"),
            P("mp"),
            P(None, "mp"),
            P("dp", "mp"),
            P("dp", None),
        ),
        out_specs=(P("dp", "mp"), P("dp", "mp"), P(None, "mp"), P("mp"), P("mp")),
        check_vma=False,
    )
```

profile of v0, /device:TPU:0, one launch (start us, length us, event | category | flops | bytes accessed | tf_op | source)
XLA Modules:
  0.0 271.8 jit_solution(12758320156787033243)
XLA Ops:
  9.7 5.8 %psum.56 = f32[1024]{0:T(1024)S(1)} all-reduce(f32[1024]{0:T(1024)S(1)} %convert_reduce_fusion), channel_id=1, replica_groups=mesh['dp'=16,'mp'=2] {'mp'}, use_global_device_ids=true, to_apply=%region_1.0 | all-reduce | flops 1024 | bytes 8192 | tf_op jit(solution)/shard_map/psum | solution.py:31
  16.3 2.0 fusion.21
  18.3 5.0 %psum.57 = f32[1024]{0:T(1024)S(1)} all-reduce(f32[1024]{0:T(1024)S(1)} %fusion.21), channel_id=1, replica_groups=mesh['dp'=16,'mp'=2] {'mp'}, use_global_device_ids=true, to_apply=%region_3.0 | all-reduce | flops 1024 | bytes 8192 | tf_op jit(solution)/shard_map/psum | solution.py:33
  25.7 2.0 copy.18
  28.8 4.1 %select_maximum_fusion.1 = f32[4,8,66,768]{3,0,2,1:T(4,128)} fusion(f32[4,7,30,768]{3,0,2,1:T(4,128)S(1)} %slice.4, f32[4,8,36,768]{3,0,2,1:T(4,128)S(1)} %bitcast.63), kind=kLoop, calls=%fused_computation.1 | loop fusion | flops 4866048 | bytes 12607488 | tf_op jit(solution)/shard_map/jvp()/conv_general_dilated | solution.py:11
  32.8 15.4 %broadcast_select_fusion.1 = f32[32,36,768]{2,0,1:T(8,128)S(1)} fusion(pred[32,36]{0,1:T(8,128)(4,1)S(1)} %copy-done.11, f32[4,8,66,768]{3,0,2,1:T(4,128)} %select_maximum_fusion.1, f32[31,1,768]{2,0,1:T(8,128)S(1)} %bitcast.58), kind=kOutput, calls=%fused_computation.41 | convolution fusion | flops 330006528 | bytes 10123392 | tf_op jit(solution)/shard_map/jvp()/conv_general_dilated | solution.py:11
  48.2 3.9 %copy.21 = f32[32,36,768]{2,1,0:T(8,128)} copy(f32[32,36,768]{2,0,1:T(8,128)S(1)} %broadcast_select_fusion.1) | data formatting | bytes 7077888 | tf_op jit(solution)/shard_map/jvp()/conv_general_dilated | solution.py:11
  52.2 5.2 %reshape.86 = f32[4,288,768]{2,1,0:T(8,128)} reshape(f32[32,36,768]{2,1,0:T(8,128)} %copy.21) | data formatting | bytes 7077888 | tf_op jit(solution)/shard_map/jvp()/conv_general_dilated | solution.py:11
  57.4 2.2 slice.5
  63.2 1.9 broadcast_multiply_fusion
  65.1 6.7 %fusion.26 = f32[1024,768]{1,0:T(8,128)S(1)} fusion(f32[4,256,768]{2,1,0:T(8,128)} %copy-done.3, bf16[1024,1536]{1,0:T(8,128)(2,1)} %broadcast_multiply_fusion, bf16[1536,768]{1,0:T(8,128)(2,1)} %all-gather.2.cloned.1.call-done), kind=kOutput, calls=%fused_computation.35 | convolution fusion | flops 2422210560 | bytes 11796480 | tf_op jit(solution)/shard_map/dot_general | solution.py:45
  71.9 22.5 %fusion.37 = f32[31,1,768]{2,1,0:T(1,128)S(1)} fusion(f32[4,256,768]{2,1,0:T(8,128)S(1)} %bitcast.66, f32[4,256,768]{2,1,0:T(8,128)S(1)} %bitcast.65), kind=kOutput, calls=%fused_computation.57 | convolution fusion | flops 283705344 | bytes 6386688 | tf_op jit(solution)/shard_map/transpose(jvp())/conv_general_dilated | solution.py:11
  95.1 6.7 %fusion.40 = f32[1536,768]{1,0:T(8,128)} fusion(bf16[1024,1536]{1,0:T(8,128)(2,1)} %broadcast_multiply_fusion, bf16[1024,768]{1,0:T(8,128)(2,1)S(1)} %fusion.27), kind=kOutput, calls=%fused_computation.60 | convolution fusion | flops 2415919104 | bytes 9437184 | tf_op jit(solution)/shard_map/dot_general | solution.py:63
  103.7 3.9 %copy.22 = f32[4,256,768]{2,0,1:T(4,128)S(1)} copy(f32[4,256,768]{2,1,0:T(8,128)} %bitcast.67) | data formatting | bytes 6291456 | tf_op jit(solution)/shard_map/reshape | solution.py:51
  108.7 4.1 %select_maximum_fusion = f32[4,8,66,768]{3,0,2,1:T(4,128)} fusion(f32[4,7,30,768]{3,0,2,1:T(4,128)S(1)} %slice.6, f32[4,8,36,768]{3,0,2,1:T(4,128)S(1)} %bitcast.61), kind=kLoop, calls=%fused_computation | loop fusion | flops 4866048 | bytes 12607488 | tf_op jit(solution)/shard_map/transpose(jvp())/conv_general_dilated | solution.py:11
  112.8 15.4 %broadcast_select_fusion = f32[32,36,768]{2,0,1:T(8,128)S(1)} fusion(pred[32,36]{0,1:T(8,128)(4,1)S(1)} %copy-done.11, f32[4,8,66,768]{3,0,2,1:T(4,128)} %select_maximum_fusion, f32[31,768,1]{1,0,2:T(8,128)S(1)} %bitcast.59), kind=kOutput, calls=%fused_computation.40 | convolution fusion | flops 330006528 | bytes 10123392 | tf_op jit(solution)/shard_map/transpose(jvp())/conv_general_dilated | solution.py:11
  128.2 4.0 %copy.25 = f32[32,36,768]{2,1,0:T(8,128)} copy(f32[32,36,768]{2,0,1:T(8,128)S(1)} %broadcast_select_fusion) | data formatting | bytes 7077888 | tf_op jit(solution)/shard_map/transpose(jvp())/conv_general_dilated | solution.py:11
  132.2 4.8 %reshape.93 = f32[4,288,768]{2,1,0:T(8,128)} reshape(f32[32,36,768]{2,1,0:T(8,128)} %copy.25) | data formatting | bytes 7077888 | tf_op jit(solution)/shard_map/transpose(jvp())/conv_general_dilated | solution.py:11
  137.0 2.7 multiply_reduce_fusion.1
  139.7 1.8 copy-done.2
  143.1 33.3 %all-reduce = (f32[]{:T(128)}, f32[768]{0:T(1024)S(1)}, f32[768]{0:T(1024)S(1)}) all-reduce(f32[]{:T(128)S(6)} %convert_element_type.46, f32[768]{0:T(1024)S(1)} %get-tuple-element.5, f32[768]{0:T(1024)S(1)} %get-tuple-element.7), channel_id=1, replica_groups=mesh['dp'=16,'mp'=2] {'dp'}, use_global_device_ids=true, to_apply=%region_9.0 | all-reduce | flops 1537 | bytes 12296 | tf_op jit(solution)/shard_map/psum | solution.py:67
  177.1 5.0 %all-reduce.1 = (f32[1024]{0:T(1024)S(1)}, f32[1024]{0:T(1024)S(1)}) all-reduce(f32[1024]{0:T(1024)S(1)} %get-tuple-element.6, f32[1024]{0:T(1024)S(1)} %bitcast.74), channel_id=1, replica_groups=mesh['dp'=16,'mp'=2] {'mp'}, use_global_device_ids=true, to_apply=%region_7.0 | all-reduce | flops 2048 | bytes 16384 | tf_op jit(solution)/shard_map/psum | solution.py:56
  182.7 4.0 %fusion.19 = bf16[1024,768]{1,0:T(8,128)(2,1)} fusion(bf16[1024,768]{1,0:T(8,128)(2,1)S(1)} %copy-done.1, f32[4,256,768]{2,1,0:T(8,128)} %copy-done.2, f32[]{:T(128)S(6)} %mul_shard_map.3, f32[1024]{0:T(1024)S(1)} %get-tuple-element.19, f32[1024]{0:T(1024)S(1)} %get-tuple-element.20, f32[1024]{0:T(1024)S(1)} %bitcast.72, f32[768]{0:T(1024)S(1)} %copy-done.8, ...), kind=kLoop, calls=%fused_computation.24 | loop fusion | flops 10223616 | bytes 7887880 | tf_op jit(solution)/shard_map/convert_element_type | solution.py:79
  188.3 74.8 %reduce-scatter.2.cloned.1.call-done = f32[96,768]{1,0:T(8,128)} async-done(((f32[1536,768]{1,0:T(8,128)}), f32[96,768]{1,0:T(8,128)}) %reduce-scatter.2.cloned.1.call-update) | async-done | bytes 294928 | tf_op jit(solution)/shard_map/reduce_scatter | solution.py:66
  (51 shorter events, 18.8 us)
Async XLA Ops:
  7.2 25.7 %copy-start = (f32[31,768]{1,0:T(8,128)S(1)}, f32[31,768]{1,0:T(8,128)}, u32[]{:S(2)}) copy-start(f32[31,768]{1,0:T(8,128)} %param.11) | copy-start | bytes 285700
  7.2 16.1 %copy-start.1 = (bf16[1024,768]{1,0:T(8,128)(2,1)S(1)}, bf16[1024,768]{1,0:T(8,128)(2,1)}, u32[]{:S(2)}) copy-start(bf16[1024,768]{1,0:T(8,128)(2,1)} %param.7) | copy-start | bytes 4718596
  7.2 16.1 %copy-start.8 = (f32[768]{0:T(1024)S(1)}, f32[768]{0:T(1024)}, u32[]{:S(2)}) copy-start(f32[768]{0:T(1024)} %param.9) | copy-start | bytes 9220
  7.2 16.1 %copy-start.9 = (f32[768]{0:T(1024)S(1)}, f32[768]{0:T(1024)}, u32[]{:S(2)}) copy-start(f32[768]{0:T(1024)} %param.10) | copy-start | bytes 9220
  7.2 57.9 %all-gather.2.cloned.1.call-start = ((), (), s32[]{:S(2)}) async-start(), calls=%async_computation.1 | async-start | bytes 2506752 | tf_op jit(solution)/shard_map/all_gather | solution.py:47
  7.9 178.8 %all-reduce.4.cloned.1.call-start = ((), (), s32[]{:S(2)}) async-start(), calls=%async_computation.3 | async-start | bytes 196608 | tf_op jit(solution)/shard_map/psum | solution.py:67
  24.0 1.7 copy-start.4
  28.8 4.1 %copy-start.11 = (pred[32,36]{0,1:T(8,128)(4,1)S(1)}, pred[32,36]{0,1:T(8,128)(4,1)}, u32[]{:S(2)}) copy-start(pred[32,36]{0,1:T(8,128)(4,1)} %constant.39) | copy-start | bytes 3460
  59.5 1.7 copy-start.3
  61.3 1.9 copy-start.6
  65.1 6.8 %copy-start.5 = (f32[1024,768]{1,0:T(8,128)S(1)}, f32[1024,768]{1,0:T(8,128)}, u32[]{:S(2)}) copy-start(f32[1024,768]{1,0:T(8,128)} %copy-done.4) | copy-start | bytes 9437188
  71.8 22.5 %copy-start.7 = (f32[1024,768]{1,0:T(8,128)}, f32[1024,768]{1,0:T(8,128)S(1)}, u32[]{:S(2)}) copy-start(f32[1024,768]{1,0:T(8,128)S(1)} %fusion.26) | copy-start | bytes 9437188
  95.1 168.1 %reduce-scatter.2.cloned.1.call-start = ((), (), s32[]{:S(2)}) async-start(), calls=%async_computation.2 | async-start | bytes 5013504 | tf_op jit(solution)/shard_map/reduce_scatter | solution.py:66
  101.8 0.7 copy-start.10
  139.7 1.8 copy-start.2
Sparse Core Ops, SparseCore 0:
  10.3 44.9 all-gather.1
  95.2 88.9 all-reduce.3
  188.5 74.5 reduce-scatter.1
where the time goes:
time: 277 us; the launch traced here: 272 us
  waiting for transfers between devices  75.6 us (27%)
  matrix products  66.8 us (24%)
  blocking collectives  49.1 us (18%)
  local copies, waits for them, and re-layouts  35.5 us (13%)
  other arithmetic  29 us (10%)
  between operations  15.7 us (6%)
    reduce_scatter x1, waiting for transfers between devices, body(): weight_grad = lax.psum_scatter(term, 'dp', scatter_dimension=0, tiled=True)  74.8 us
    conv_general_dilated x3, matrix products, depthwise(): lax.conv_general_dilated(inputs, taps[:, None, :], (1,), [(half, half)],...  53.4 us
    psum x1, blocking collectives, body(): lax.psum((kernel_part, gain_part, bias_part, local_total), 'dp')  33.3 us
    conv_general_dilated x7, local copies, waits for them, and re-layouts, depthwise(): lax.conv_general_dilated(inputs, taps[:, None, :], (1,), [(half, half)],...  20.9 us
    conv_general_dilated x2, other arithmetic, depthwise(): lax.conv_general_dilated(inputs, taps[:, None, :], (1,), [(half, half)],...  8.17 us
    unnamed x27, local copies, waits for them, and re-layouts  7.5 us
    dot_general x1, matrix products, body(): jnp.dot(columns, lax.all_gather(point_weight, 'dp', axis=0, tiled=True),...  6.73 us
    dot_general x1, matrix products, body(): lax.dot_general(columns, activation, (((0,), (0,)), ((), ())), preferred_...  6.69 us
  transfers between devices with their start and end apart: 3, of which 1 were waited for; matrix products, arithmetic and copies ran while one was open for 34% of the time, Pallas kernels for 0%

commit v1 on v0

--- a/solution.py
+++ b/solution.py
@@ -1,9 +1,17 @@
+import functools
+
 import jax
 import jax.numpy as jnp
 from jax import lax
+from jax.experimental import pallas as pl
+from jax.experimental.pallas import tpu as pltpu
 from jax.sharding import PartitionSpec as P
 
 epsilon = 1e-05
+LANES = 128
+CHUNK = 64
+F32 = jnp.float32
+BF16 = jnp.bfloat16
 
 
 def depthwise(inputs, taps):
@@ -19,7 +27,7 @@
     )
 
 
-def body(frames_in, lengths, ln_gain, ln_bias, kernel, point_weight, target):
+def plain_body(frames_in, lengths, ln_gain, ln_bias, kernel, point_weight, target):
     tok_rows, chan_count = frames_in.shape
     utt_count = lengths.shape[0]
     frame_count = tok_rows // utt_count
@@ -41,9 +49,8 @@
     gate_sig = jax.nn.sigmoid(pre_act)
     activation = (pre_act * gate_sig).astype(jnp.bfloat16)
     cotangent = target * valid_mask.astype(jnp.bfloat16)
-    columns = cotangent
     act_grad = jnp.dot(
-        columns,
+        cotangent,
         lax.all_gather(point_weight, "dp", axis=0, tiled=True),
         preferred_element_type=jnp.float32,
     )
@@ -59,28 +66,577 @@
     norm_grad = inv_std * (
         hat_grad - hat_sum[:, None] / full_width - normed * (hat_dot[:, None] / full_width)
     )
-    columns = cotangent
     term = lax.dot_general(
-        columns, activation, (((0,), (0,)), ((), ())), preferred_element_type=jnp.float32
+        cotangent, activation, (((0,), (0,)), ((), ())), preferred_element_type=jnp.float32
     )
     weight_grad = lax.psum_scatter(term, "dp", scatter_dimension=0, tiled=True)
     kernel_sum, gain_sum, bias_sum, frame_total = lax.psum(
         (kernel_part, gain_part, bias_part, local_total), "dp"
     )
     inverse = 1.0 / frame_total
-    kernel_grad = kernel_sum * inverse
-    gain_grad = gain_sum * inverse
-    bias_grad = bias_sum * inverse
-    weight_grad = weight_grad * inverse
     own_grad = lax.dynamic_slice_in_dim(
         cotangent, lax.axis_index("mp") * chan_count, chan_count, 1
     ).astype(jnp.float32)
     slot_total = tok_rows * lax.axis_size("dp")
     frames_grad = ((own_grad + norm_grad) * (slot_total * inverse)).astype(jnp.bfloat16)
-    return (frames_grad, weight_grad, kernel_grad, gain_grad, bias_grad)
+    return (
+        frames_grad,
+        weight_grad * inverse,
+        kernel_sum * inverse,
+        gain_sum * inverse,
+        bias_sum * inverse,
+    )
+
+
+def rcopy(src, dst, sends, recvs, at, peer):
+    return pltpu.make_async_remote_copy(
+        src_ref=src,
+        dst_ref=dst,
+        send_sem=sends.at[at],
+        recv_sem=recvs.at[at],
+        device_id=peer,
+        device_id_type=pl.DeviceIdType.MESH,
+    )
+
+
+def mp_peers(mp):
+    me_dp, me_mp = lax.axis_index("dp"), lax.axis_index("mp")
+    return [(me_dp, lax.rem(me_mp + s, mp)) for s in range(1, mp)]
+
+
+def dp_bits(stages):
+    me_dp, me_mp = lax.axis_index("dp"), lax.axis_index("mp")
+    bits = [(me_dp // (1 << s)) % 2 for s in range(stages)]
+    peers = [(me_dp + (1 << s) * (1 - 2 * bits[s]), me_mp) for s in range(stages)]
+    return bits, peers
+
+
+def greet(peers):
+    barrier = pltpu.get_barrier_semaphore()
+    for peer in peers:
+        pl.semaphore_signal(
+            barrier, inc=1, device_id=peer, device_id_type=pl.DeviceIdType.MESH
+        )
+    pl.semaphore_wait(barrier, len(peers))
+
+
+def eye_mask():
+    shape = (LANES, LANES)
+    return lax.broadcasted_iota(jnp.int32, shape, 0) == lax.broadcasted_iota(jnp.int32, shape, 1)
+
+
+def to_row(column, eye):
+    return jnp.sum(jnp.where(eye, column, 0.0), axis=0, keepdims=True)
+
+
+def to_column(row, eye):
+    return jnp.sum(jnp.where(eye, row, 0.0), axis=1, keepdims=True)
+
+
+def lane_at(c):
+    return pl.ds(pl.multiple_of(c * LANES, LANES), LANES)
+
+
+def rows_at(start, size, unit):
+    return pl.ds(pl.multiple_of(start, unit), size)
+
+
+def valid_rows(len_ref, u, start, size):
+    position = start + lax.broadcasted_iota(jnp.int32, (size, LANES), 0)
+    return position < len_ref[u]
+
+
+def forward_kernel(
+    mp, utts, frames, taps, pad,
+    len_ref, x_ref, gain_ref, bias_ref, tap_ref, target_ref,
+    masked_ref, pre_ref, act_ref, cot_ref, mean_ref, rstd_ref,
+    stat, got, sends, recvs,
+):
+    tok, chan = x_ref.shape
+    groups = tok // LANES
+    blocks = chan // LANES
+    span = frames + 2 * pad
+    peers = mp_peers(mp)
+    greet(peers)
+    eye = eye_mask()
+
+    def stats(g, _):
+        values = x_ref[rows_at(g * LANES, LANES, LANES), :].astype(F32)
+        local = jnp.sum(values, axis=1, keepdims=True) * (1.0 / chan)
+        off = values - local
+        squares = jnp.sum(off * off, axis=1, keepdims=True)
+        stat[0, pl.ds(g, 1), :] = to_row(local, eye)
+        stat[1, pl.ds(g, 1), :] = to_row(squares, eye)
+        return 0
+
+    lax.fori_loop(0, groups, stats, 0)
+    copies = [
+        rcopy(stat, got.at[s], sends, recvs, s, peer) for s, peer in enumerate(peers)
+    ]
+    for copy in copies:
+        copy.start()
+
+    def mask_target(i, _):
+        u, part = i // (frames // CHUNK), i % (frames // CHUNK)
+        rows = rows_at(i * CHUNK, CHUNK, CHUNK)
+        valid = valid_rows(len_ref, u, part * CHUNK, CHUNK)
+        for c in range(target_ref.shape[1] // LANES):
+            lanes = pl.ds(c * LANES, LANES)
+            block = target_ref[rows, lanes].astype(F32)
+            cot_ref[rows, lanes] = jnp.where(valid, block, 0.0).astype(BF16)
+        return 0
+
+    lax.fori_loop(0, tok // CHUNK, mask_target, 0)
+
+    def clear(i, _):
+        c, u = i // utts, i % utts
+        edge = jnp.zeros((pad, LANES), F32)
+        masked_ref[c, rows_at(u * span, pad, pad), :] = edge
+        masked_ref[c, rows_at(u * span + pad + frames, pad, pad), :] = edge
+        return 0
+
+    lax.fori_loop(0, blocks * utts, clear, 0)
+    for copy in copies:
+        copy.wait()
+    mean = stat[0]
+    for s in range(mp - 1):
+        mean = mean + got[s, 0]
+    mean = mean * (1.0 / mp)
+    squares = stat[1] + chan * (stat[0] - mean) * (stat[0] - mean)
+    for s in range(mp - 1):
+        squares = squares + (got[s, 1] + chan * (got[s, 0] - mean) * (got[s, 0] - mean))
+    stat[0] = mean
+    stat[1] = lax.rsqrt(squares * (1.0 / (chan * mp)) + epsilon)
+
+    def spread(g, _):
+        rows = rows_at(g * LANES, LANES, LANES)
+        shape = (LANES, LANES)
+        mean_ref[rows, :] = jnp.broadcast_to(to_column(stat[0, pl.ds(g, 1), :], eye), shape)
+        rstd_ref[rows, :] = jnp.broadcast_to(to_column(stat[1, pl.ds(g, 1), :], eye), shape)
+        return 0
+
+    lax.fori_loop(0, groups, spread, 0)
+
+    def block(c, _):
+        lanes = lane_at(c)
+        gain, bias = gain_ref[c], bias_ref[c]
+
+        def norm(i, _):
+            u, part = i // (frames // CHUNK), i % (frames // CHUNK)
+            rows = rows_at(i * CHUNK, CHUNK, CHUNK)
+            values = x_ref[rows, lanes].astype(F32)
+            normed = (values - mean_ref[rows, :]) * rstd_ref[rows, :]
+            valid = valid_rows(len_ref, u, part * CHUNK, CHUNK)
+            masked_ref[c, rows_at(u * span + pad + part * CHUNK, CHUNK, 16), :] = jnp.where(
+                valid, normed * gain + bias, 0.0
+            )
+            return 0
+
+        lax.fori_loop(0, tok // CHUNK, norm, 0)
+
+        def conv(i, _):
+            u, part = i // (frames // CHUNK), i % (frames // CHUNK)
+            rows = rows_at(i * CHUNK, CHUNK, CHUNK)
+            base = u * span + part * CHUNK
+            shift = pad - (taps - 1) // 2
+            total = jnp.zeros((CHUNK, LANES), F32)
+            for b in range(8):
+                ks = [k for k in range(taps) if (k + shift) % 8 == b]
+                reach = 8 * max((k + shift) // 8 for k in ks)
+                slab = masked_ref[c, pl.ds(base + b, CHUNK + reach), :]
+                for k in ks:
+                    at = (k + shift) // 8 * 8
+                    total = total + tap_ref[c, pl.ds(k, 1), :] * slab[at:at + CHUNK]
+            pre_ref[c, rows, :] = total
+            act_ref[rows, lanes] = (total * jax.nn.sigmoid(total)).astype(BF16)
+            return 0
+
+        lax.fori_loop(0, tok // CHUNK, conv, 0)
+        return 0
+
+    lax.fori_loop(0, blocks, block, 0)
+
+
+def backward_kernel(
+    mp, stages, utts, frames, taps, pad,
+    len_ref, x_ref, gain_ref, tap_ref, weight_ref,
+    masked_ref, pre_ref, act_ref, cot_ref, mean_ref, rstd_ref,
+    out_ref, wgrad_ref, small_ref,
+    term, core_got, a1, a2, a3, b1, b2, b3,
+    pgrad, hat, hat_sum, hat_dot, tap_acc, stat, got, count, count_got, small, small_got,
+    core_s, core_r, ring_s, ring_r, hat_s, hat_r, cnt_s, cnt_r, sm_s, sm_r,
+):
+    tok, chan = x_ref.shape
+    width = cot_ref.shape[1]
+    groups = tok // LANES
+    blocks = chan // LANES
+    span = frames + 2 * pad
+    per_utt = frames // CHUNK
+    half = chan // 2
+    out_rows = wgrad_ref.shape[0]
+    highs = term.shape[0]
+    row_peers = mp_peers(mp)
+    bits, peers = dp_bits(stages)
+    greet(peers + row_peers)
+    core, why, zlo, zhi = bits
+    eye = eye_mask()
+
+    total = len_ref[0]
+    for u in range(1, utts):
+        total = total + len_ref[u]
+    count[0] = jnp.full((8, LANES), total, jnp.int32).astype(F32)
+    cnt = [
+        rcopy(count.at[s], count_got.at[s], cnt_s, cnt_r, s, peers[s]) for s in range(stages)
+    ]
+    cnt[0].start()
+    core_copies = []
+    group_rows = width // highs
+    for g in range(highs):
+        product = lax.dot_general(
+            cot_ref[:, g * group_rows:(g + 1) * group_rows],
+            act_ref[...],
+            (((0,), (0,)), ((), ())),
+            preferred_element_type=F32,
+        )
+        for y in range(2):
+            for k in range(2):
+                at = (2 * y + k) * out_rows
+                term[g, y, k] = product[at:at + out_rows]
+        copy = rcopy(
+            term.at[g, :, 1 - core], core_got.at[g], core_s, core_r, g, peers[0]
+        )
+        copy.start()
+        core_copies.append(copy)
+        cnt[g].wait()
+        count[g + 1] = count[g] + count_got[g]
+        if g + 1 < stages:
+            cnt[g + 1].start()
+    inverse = 1.0 / count[stages]
+
+    def clear(i, _):
+        c, u = i // utts, i % utts
+        edge = jnp.zeros((pad, LANES), F32)
+        pgrad[c, rows_at(u * span, pad, pad), :] = edge
+        pgrad[c, rows_at(u * span + pad + frames, pad, pad), :] = edge
+        return 0
+
+    lax.fori_loop(0, blocks * utts, clear, 0)
+
+    def act_grad(u, _):
+        rows = rows_at(u * frames, frames, frames)
+        product = jnp.dot(cot_ref[rows, :], weight_ref[...], preferred_element_type=F32)
+        for c in range(blocks):
+            pre = pre_ref[c, rows, :]
+            gate = jax.nn.sigmoid(pre)
+            grad = product[:, c * LANES:(c + 1) * LANES]
+            pgrad[c, rows_at(u * span + pad, frames, 16), :] = (
+                grad * gate * (1.0 + pre * (1.0 - gate))
+            )
+        return 0
+
+    lax.fori_loop(0, utts, act_grad, 0)
+
+    for copy in core_copies:
+        copy.wait()
+
+    def join_core(i, _):
+        g, y = i // 2, i % 2
+        core_got[g, y] = core_got[g, y] + term[g, y, core]
+        return 0
+
+    lax.fori_loop(0, highs * 2, join_core, 0)
+    left, right = pl.ds(0, half), pl.ds(half, half)
+
+    copy_a1 = rcopy(core_got.at[:, 1 - why, :, left], a1, ring_s, ring_r, 0, peers[1])
+    copies_b1 = [
+        rcopy(
+            core_got.at[2 * h + 1 - zlo, :, :, right], b1.at[h], ring_s, ring_r, 1 + h, peers[2]
+        )
+        for h in range(2)
+    ]
+    copies_a2 = [
+        rcopy(a1.at[2 * h + 1 - zlo], a2.at[h], ring_s, ring_r, 3 + h, peers[2])
+        for h in range(2)
+    ]
+    copy_b2 = rcopy(b1.at[1 - zhi], b2, ring_s, ring_r, 5, peers[3])
+    copy_a3 = rcopy(a2.at[1 - zhi], a3, ring_s, ring_r, 6, peers[3])
+    copy_b3 = rcopy(b2.at[1 - why], b3, ring_s, ring_r, 7, peers[1])
+
+    copy_a1.start()
+    for copy in copies_b1:
+        copy.start()
+
+    def second_stage():
+        copy_a1.wait()
+        for h in range(highs):
+            a1[h] = a1[h] + core_got[h, why, :, left]
+        for copy in copies_a2:
+            copy.start()
+        for copy in copies_b1:
+            copy.wait()
+        for h in range(2):
+            for y in range(2):
+                b1[h, y] = b1[h, y] + core_got[2 * h + zlo, y, :, right]
+        copy_b2.start()
+
+    def third_stage():
+        for copy in copies_a2:
+            copy.wait()
+        for h in range(2):
+            a2[h] = a2[h] + a1[2 * h + zlo]
+        copy_a3.start()
+        copy_b2.wait()
+        for y in range(2):
+            b2[y] = b2[y] + b1[zhi, y]
+        copy_b3.start()
+
+    def last_stage():
+        scale = inverse[0:1, 0:1]
+        copy_a3.wait()
+        wgrad_ref[:, 0:half] = (a3[...] + a2[zhi]) * scale
+        copy_b3.wait()
+        wgrad_ref[:, half:chan] = (b3[...] + b2[why]) * scale
+
+    shift = pad - (taps - 1) // 2
+
+    def block(c, _):
+        lanes = lane_at(c)
+        gain = gain_ref[c]
+        tap_acc[...] = jnp.zeros_like(tap_acc)
+
+        def part_of(i, _):
+            u, part = i // per_utt, i % per_utt
+            rows = rows_at(i * CHUNK, CHUNK, CHUNK)
+            base = u * span + part * CHUNK
+            total = jnp.zeros((CHUNK, LANES), F32)
+            grads = pgrad[c, rows_at(base + pad, CHUNK, 16), :]
+            for b in range(8):
+                ks = [k for k in range(taps) if (k + shift) % 8 == b]
+                reach = 8 * max((k + shift) // 8 for k in ks)
+                slab = pgrad[c, pl.ds(base + b, CHUNK + reach), :]
+                for k in ks:
+                    at = (k + shift) // 8 * 8
+                    total = total + tap_ref[c, pl.ds(taps - 1 - k, 1), :] * slab[at:at + CHUNK]
+            for b in range(8):
+                ks = [k for k in range(taps) if (k + shift) % 8 == b]
+                reach = 8 * max((k + shift) // 8 for k in ks)
+                slab = masked_ref[c, pl.ds(base + b, CHUNK + reach), :]
+                for k in ks:
+                    at = (k + shift) // 8 * 8
+                    part_sum = grads * slab[at:at + CHUNK]
+                    tap_acc[k] += jnp.sum(part_sum.reshape(CHUNK // 8, 8, LANES), axis=0)
+            valid = valid_rows(len_ref, u, part * CHUNK, CHUNK)
+            masked_grad = jnp.where(valid, total, 0.0)
+            normed = (x_ref[rows, lanes].astype(F32) - mean_ref[rows, :]) * rstd_ref[rows, :]
+            scaled = masked_grad * normed
+            tap_acc[taps] += jnp.sum(scaled.reshape(CHUNK // 8, 8, LANES), axis=0)
+            tap_acc[taps + 1] += jnp.sum(masked_grad.reshape(CHUNK // 8, 8, LANES), axis=0)
+            grad = masked_grad * gain
+            hat[c, rows, :] = grad
+            hat_sum[rows, :] += grad
+            hat_dot[rows, :] += scaled * gain
+            return 0
+
+        lax.fori_loop(0, tok // CHUNK, part_of, 0)
+        sums = jnp.sum(tap_acc[...], axis=1)
+        small[0, :, lanes] = sums
+        return 0
+
+    def reset(i, _):
+        rows = rows_at(i * CHUNK, CHUNK, CHUNK)
+        hat_sum[rows, :] = jnp.zeros((CHUNK, LANES), F32)
+        hat_dot[rows, :] = jnp.zeros((CHUNK, LANES), F32)
+        return 0
+
+    lax.fori_loop(0, tok // CHUNK, reset, 0)
+    cut = [0, blocks // 2, blocks - blocks // 6, blocks]
+    lax.fori_loop(cut[0], cut[1], block, 0)
+    second_stage()
+    lax.fori_loop(cut[1], cut[2], block, 0)
+    third_stage()
+    lax.fori_loop(cut[2], cut[3], block, 0)
+
+    def collect(g, _):
+        rows = rows_at(g * LANES, LANES, LANES)
+        stat[0, pl.ds(g, 1), :] = to_row(jnp.sum(hat_sum[rows, :], axis=1, keepdims=True), eye)
+        stat[1, pl.ds(g, 1), :] = to_row(jnp.sum(hat_dot[rows, :], axis=1, keepdims=True), eye)
+        return 0
+
+    sm = [
+        rcopy(small.at[s], small_got.at[s], sm_s, sm_r, s, peers[s]) for s in range(stages)
+    ]
+    sm[0].start()
+    lax.fori_loop(0, groups, collect, 0)
+    hats = [
+        rcopy(stat, got.at[s], hat_s, hat_r, s, peer) for s, peer in enumerate(row_peers)
+    ]
+    for copy in hats:
+        copy.start()
+    sm[0].wait()
+    small[1] = small[0] + small_got[0]
+    sm[1].start()
+    for copy in hats:
+        copy.wait()
+    for j in range(2):
+        joined = stat[j]
+        for s in range(mp - 1):
+            joined = joined + got[s, j]
+        stat[j] = joined * (1.0 / width)
+
+    def spread(g, _):
+        rows = rows_at(g * LANES, LANES, LANES)
+        shape = (LANES, LANES)
+        hat_sum[rows, :] = jnp.broadcast_to(to_column(stat[0, pl.ds(g, 1), :], eye), shape)
+        hat_dot[rows, :] = jnp.broadcast_to(to_column(stat[1, pl.ds(g, 1), :], eye), shape)
+        return 0
+
+    lax.fori_loop(0, groups, spread, 0)
+    own = lax.axis_index("mp") * blocks
+    slots = (tok * (1 << stages)) * inverse[0:1, :]
+
+    def finish(i, _):
+        rows = rows_at(i * CHUNK, CHUNK, CHUNK)
+        mean, rstd = mean_ref[rows, :], rstd_ref[rows, :]
+        sums, dots = hat_sum[rows, :], hat_dot[rows, :]
+        for c in range(blocks):
+            lanes = pl.ds(c * LANES, LANES)
+            normed = (x_ref[rows, lanes].astype(F32) - mean) * rstd
+            grad = rstd * (hat[c, rows, :] - sums - normed * dots)
+            direct = cot_ref[rows, lane_at(own + c)].astype(F32)
+            out_ref[rows, lanes] = ((direct + grad) * slots).astype(BF16)
+        return 0
+
+    parts = tok // CHUNK
+    marks = [parts * s // (stages - 1) for s in range(stages)]
+    for s in range(1, stages):
+        lax.fori_loop(marks[s - 1], marks[s], finish, 0)
+        sm[s].wait()
+        small[s + 1] = small[s] + small_got[s]
+        if s + 1 < stages:
+            sm[s + 1].start()
+    small_ref[...] = small[stages] * inverse[0:1, 0:1]
+    last_stage()
+
+
+def fast_body(dp, mp, frames_in, lengths, ln_gain, ln_bias, kernel, point_weight, target):
+    tok, chan = frames_in.shape
+    utts = lengths.shape[0]
+    frames = tok // utts
+    width = target.shape[1]
+    taps = kernel.shape[0]
+    pad = 16
+    blocks = chan // LANES
+    stages = dp.bit_length() - 1
+    groups = tok // LANES
+    span = utts * (frames + 2 * pad)
+    out_rows = width // dp
+    highs = dp // 4
+    half = chan // 2
+    gathered = lax.all_gather(point_weight, "dp", axis=0, tiled=True)
+    gain = ln_gain.reshape(blocks, 1, LANES)
+    bias = ln_bias.reshape(blocks, 1, LANES)
+    tap_blocks = kernel.reshape(taps, blocks, LANES).transpose(1, 0, 2)
+    vmem = pl.BlockSpec(memory_space=pltpu.VMEM)
+    smem = pl.BlockSpec(memory_space=pltpu.SMEM)
+    dma = pltpu.SemaphoreType.DMA
+    shape = jax.ShapeDtypeStruct
+    peers = max(mp - 1, 1)
+    masked, pre, act, cot, mean, rstd = pl.pallas_call(
+        functools.partial(forward_kernel, mp, utts, frames, taps, pad),
+        out_shape=(
+            shape((blocks, span, LANES), F32),
+            shape((blocks, tok, LANES), F32),
+            shape((tok, chan), BF16),
+            shape((tok, width), BF16),
+            shape((tok, LANES), F32),
+            shape((tok, LANES), F32),
+        ),
+        in_specs=[smem] + [vmem] * 5,
+        out_specs=(vmem,) * 6,
+        scratch_shapes=[
+            pltpu.VMEM((2, groups, LANES), F32),
+            pltpu.VMEM((peers, 2, groups, LANES), F32),
+            dma((peers,)),
+            dma((peers,)),
+        ],
+        compiler_params=pltpu.CompilerParams(
+            collective_id=0, has_side_effects=True, vmem_limit_bytes=40 * 2**20
+        ),
+        cost_estimate=pl.CostEstimate(
+            flops=40 * tok * chan * taps, bytes_accessed=24 * tok * chan, transcendentals=tok * chan
+        ),
+        name="forward",
+    )(lengths, frames_in, gain, bias, tap_blocks, target)
+    side = (taps + 2 + 7) // 8 * 8
+    frames_grad, weight_grad, small = pl.pallas_call(
+        functools.partial(backward_kernel, mp, stages, utts, frames, taps, pad),
+        out_shape=(
+            shape((tok, chan), BF16),
+            shape((out_rows, chan), F32),
+            shape((side, chan), F32),
+        ),
+        in_specs=[smem] + [vmem] * 10,
+        out_specs=(vmem,) * 3,
+        scratch_shapes=[
+            pltpu.VMEM((highs, 2, 2, out_rows, chan), F32),
+            pltpu.VMEM((highs, 2, out_rows, chan), F32),
+            pltpu.VMEM((highs, out_rows, half), F32),
+            pltpu.VMEM((2, out_rows, half), F32),
+            pltpu.VMEM((out_rows, half), F32),
+            pltpu.VMEM((2, 2, out_rows, half), F32),
+            pltpu.VMEM((2, out_rows, half), F32),
+            pltpu.VMEM((out_rows, half), F32),
+            pltpu.VMEM((blocks, span, LANES), F32),
+            pltpu.VMEM((blocks, tok, LANES), F32),
+            pltpu.VMEM((tok, LANES), F32),
+            pltpu.VMEM((tok, LANES), F32),
+            pltpu.VMEM((side, 8, LANES), F32),
+            pltpu.VMEM((2, groups, LANES), F32),
+            pltpu.VMEM((peers, 2, groups, LANES), F32),
+            pltpu.VMEM((stages + 1, 8, LANES), F32),
+            pltpu.VMEM((stages, 8, LANES), F32),
+            pltpu.VMEM((stages + 1, side, chan), F32),
+            pltpu.VMEM((stages, side, chan), F32),
+            dma((highs,)),
+            dma((highs,)),
+            dma((8,)),
+            dma((8,)),
+            dma((peers,)),
+            dma((peers,)),
+            dma((stages,)),
+            dma((stages,)),
+            dma((stages,)),
+            dma((stages,)),
+        ],
+        compiler_params=pltpu.CompilerParams(
+            collective_id=1, has_side_effects=True, vmem_limit_bytes=56 * 2**20
+        ),
+        name="backward",
+    )(lengths, frames_in, gain, tap_blocks, gathered, masked, pre, act, cot, mean, rstd)
+    return (frames_grad, weight_grad, small[:taps], small[taps], small[taps + 1])
 
 
 def solution(mesh):
+    dp, mp = mesh.shape["dp"], mesh.shape["mp"]
+
+    def body(frames_in, lengths, ln_gain, ln_bias, kernel, point_weight, target):
+        args = (frames_in, lengths, ln_gain, ln_bias, kernel, point_weight, target)
+        tok, chan = frames_in.shape
+        frames = tok // lengths.shape[0]
+        width = target.shape[1]
+        fits = (
+            dp == 2**4
+            and mp > 1
+            and chan % (2 * LANES) == 0
+            and tok % LANES == 0
+            and frames % CHUNK == 0
+            and width % (dp // 4 * LANES) == 0
+            and width % (dp * 8) == 0
+            and kernel.shape[0] % 2 == 1
+            and kernel.shape[0] <= 31
+        )
+        return fast_body(dp, mp, *args) if fits else plain_body(*args)
+
     return jax.shard_map(
         body,
         mesh=mesh,

time: 277 us -> 141 us (0.51); the launches traced: 272 us -> 141 us
  Pallas kernels: 0 us -> 94 us
  matrix products: 66.8 us -> 0 us
  waiting for transfers between devices: 75.6 us -> 14.2 us
  blocking collectives: 49.1 us -> 0 us
  other arithmetic: 29 us -> 0 us
  local copies, waits for them, and re-layouts: 35.5 us -> 18.8 us
    pallas_call x0 -> x2, Pallas kernels: none -> 94 us  [the longest x1 72.7 us: fast_body(): pl.pallas_call(functools.partial(backward_kernel, mp, stages, utts, frame...]
    reduce_scatter x1 -> x0, waiting for transfers between devices: 74.8 us -> none  [body(): weight_grad = lax.psum_scatter(term, 'dp', scatter_dimension=0, tiled=True)]
    conv_general_dilated x3 -> x0, matrix products: 53.4 us -> none  [depthwise(): lax.conv_general_dilated(inputs, taps[:, None, :], (1,), [(half, half)],...]
    psum x4 -> x0, blocking collectives: 49.1 us -> none  [the longest x1 33.3 us: body(): lax.psum((kernel_part, gain_part, bias_part, local_total), 'dp')]
    conv_general_dilated x7 -> x0, local copies, waits for them, and re-layouts: 20.9 us -> none  [depthwise(): lax.conv_general_dilated(inputs, taps[:, None, :], (1,), [(half, half)],...]
    all_gather x1, waiting for transfers between devices: 0.01 us -> 13.5 us  [fast_body(): gathered = lax.all_gather(point_weight, 'dp', axis=0, tiled=True)]
    dot_general x2 -> x0, matrix products: 13.4 us -> none  [the longest x1 6.73 us: body(): jnp.dot(columns, lax.all_gather(point_weight, 'dp', axis=0, tiled=True),...]
    reduce_sum x5 -> x0, other arithmetic: 8.68 us -> none  [the longest x1 2.7 us: body(): bias_part = jnp.sum(masked_grad, axis=0)]
  transfers between devices with their start and end apart: 3 -> 1, of which waited for: 1 -> 1; matrix products, arithmetic and copies ran while one was open for 34% -> 2% of each run, Pallas kernels for 0% -> 15%
where the time goes in v1:
time: 141 us
  Pallas kernels  94 us (67%)
  local copies, waits for them, and re-layouts  18.8 us (13%)
  waiting for transfers between devices  14.2 us (10%)
  between operations  14.1 us (10%)
    pallas_call x1, Pallas kernels, fast_body(): pl.pallas_call(functools.partial(backward_kernel, mp, stages, utts, frame...  72.7 us
    pallas_call x1, Pallas kernels, fast_body(): pl.pallas_call(functools.partial(forward_kernel, mp, utts, frames, taps,...  21.3 us
    unnamed x24, local copies, waits for them, and re-layouts  13.5 us
    all_gather x1, waiting for transfers between devices, fast_body(): gathered = lax.all_gather(point_weight, 'dp', axis=0, tiled=True)  13.5 us
  transfers between devices with their start and end apart: 1, of which 1 were waited for; matrix products, arithmetic and copies ran while one was open for 2% of the time, Pallas kernels for 15%

profile of v1, /device:TPU:0, one launch (start us, length us, event | category | flops | bytes accessed | tf_op | source)
XLA Modules:
  0.0 141.1 jit_solution(9784864443073631505)
XLA Ops:
  7.2 0.0 all-gather.2.cloned.1.call-start
  7.2 0.7 all-gather.2.cloned.1.call-update
  7.9 0.7 reshape.19.gain_ref
  8.6 0.7 reshape.21.bias_ref
  9.3 0.9 reshape.20
  10.2 0.0 copy-start.5
  10.2 0.0 copy-start
  10.3 1.4 %copy-done = bf16[1024,768]{1,0:T(8,128)(2,1)S(1)} copy-done((bf16[1024,768]{1,0:T(8,128)(2,1)S(1)}, bf16[1024,768]{1,0:T(8,128)(2,1)}, u32[]{:S(2)}) %copy-start) | copy-done | bytes 1572888
  11.7 1.9 %copy-done.1 = bf16[1024,1536]{1,0:T(8,128)(2,1)S(1)} copy-done((bf16[1024,1536]{1,0:T(8,128)(2,1)S(1)}, bf16[1024,1536]{1,0:T(8,128)(2,1)}, u32[]{:S(2)}) %copy-start.1) | copy-done | bytes 3145752
  13.6 0.7 copy-done.9
  14.2 21.3 %forward.1 = (f32[6,1152,128]{2,1,0:T(8,128)}, f32[6,1024,128]{2,1,0:T(8,128)S(1)}, bf16[1024,768]{1,0:T(8,128)(2,1)S(1)}, bf16[1024,1536]{1,0:T(8,128)(2,1)S(1)...) custom-call(s32[4]{0:T(128)S(1)} %copy-done.9, bf16[1024,768]{1,0:T(8,128)(2,1)S(1)} %copy-done, ...), custom_call_target="tpu_custom_call" | custom-call | flops 975175680 | bytes 18874368 | tf_op jit(solution)/shard_map/forward/pallas_call | solution.py:544
  35.5 1.7 %copy-done.2 = f32[6,1024,128]{2,1,0:T(8,128)} copy-done((f32[6,1024,128]{2,1,0:T(8,128)}, f32[6,1024,128]{2,1,0:T(8,128)S(1)}, u32[]{:S(2)}) %copy-start.2) | copy-done | bytes 3145752
  37.2 1.7 %copy-done.3 = bf16[1024,1536]{1,0:T(8,128)(2,1)} copy-done((bf16[1024,1536]{1,0:T(8,128)(2,1)}, bf16[1024,1536]{1,0:T(8,128)(2,1)S(1)}, u32[]{:S(2)}) %copy-start.3) | copy-done | bytes 3145752
  39.0 1.1 copy-done.4
  40.1 0.8 copy-done.6
  40.9 0.8 copy-done.7
  41.7 13.5 %all-gather.2.cloned.1.call-done.weight_ref = bf16[1536,768]{1,0:T(8,128)(2,1)} async-done(((bf16[96,768]{1,0:T(8,128)(2,1)}), bf16[1536,768]{1,0:T(8,128)(2,1)}) %all-gather.2.cloned.1.call-update) | async-done | bytes 2359312 | tf_op jit(solution)/shard_map/all_gather | solution.py:535
  55.2 72.7 %backward.1 = (bf16[1024,768]{1,0:T(8,128)(2,1)}, f32[96,768]{1,0:T(8,128)}, f32[40,768]{1,0:T(8,128)}) custom-call(s32[4]{0:T(128)} %len_ref.3, bf16[1024,768]{1,0:T(8,128)(2,1)} %x_ref.3, f32[6,1,128]{2,1,0:T(1,128)} %copy-done.8, f32[6,31,128]{2,1,0:T(8,128)} %bitcast.4, bf16[1536,768]{1,0:T(8,128)(2,1)} %all-gather.2.cloned.1.call-done.weight_ref, ...), custom_call_target="tpu_custom_call" | custom-call | tf_op jit(solution)/shard_map/backward/pallas_call | solution.py:571
  127.9 0.0 copy-start.10
  127.9 1.4 %slice_reduce_fusion = (f32[768]{0:T(1024)}, f32[768]{0:T(1024)}) fusion(f32[40,768]{1,0:T(8,128)} %get-tuple-element.22), kind=kLoop, calls=%fused_computation.1 | loop fusion | bytes 12288 | tf_op jit(solution)/shard_map/slice | solution.py:616
  129.3 1.5 %slice.9 = f32[31,768]{1,0:T(8,128)} slice(f32[40,768]{1,0:T(8,128)} %get-tuple-element.22), slice={[0:31], [0:768]} | slice | bytes 190464 | tf_op jit(solution)/shard_map/slice | solution.py:616
  130.9 2.7 %copy.17 = bf16[1024,768]{1,0:T(8,128)(2,1)} copy(bf16[1024,768]{1,0:T(8,128)(2,1)} %get-tuple-element.30) | data formatting | bytes 3145728
  133.5 0.0 copy-done.10
  133.5 0.7 copy.18
  (11 shorter events, 0.0 us)
Async XLA Ops:
  7.2 48.0 %all-gather.2.cloned.1.call-start = ((), (), s32[]{:S(2)}) async-start(), calls=%async_computation | async-start | bytes 2506752 | tf_op jit(solution)/shard_map/all_gather | solution.py:535
  8.6 26.9 %copy-start.8 = (f32[6,1,128]{2,1,0:T(1,128)}, f32[6,1,128]{2,1,0:T(1,128)S(1)}, u32[]{:S(2)}) copy-start(f32[6,1,128]{2,1,0:T(1,128)S(1)} %reshape.19.gain_ref) | copy-start | bytes 9220
  10.2 25.3 %copy-start.5 = (f32[31,6,128]{2,0,1:T(8,128)}, f32[31,6,128]{2,0,1:T(8,128)S(1)}, u32[]{:S(2)}) copy-start(f32[31,6,128]{2,0,1:T(8,128)S(1)} %copy.14) | copy-start | bytes 285700
  10.2 1.4 %copy-start = (bf16[1024,768]{1,0:T(8,128)(2,1)S(1)}, bf16[1024,768]{1,0:T(8,128)(2,1)}, u32[]{:S(2)}) copy-start(bf16[1024,768]{1,0:T(8,128)(2,1)} %x_ref.3) | copy-start | bytes 4718596
  11.7 1.9 %copy-start.1 = (bf16[1024,1536]{1,0:T(8,128)(2,1)S(1)}, bf16[1024,1536]{1,0:T(8,128)(2,1)}, u32[]{:S(2)}) copy-start(bf16[1024,1536]{1,0:T(8,128)(2,1)} %target_ref.1) | copy-start | bytes 9437188
  13.6 0.7 copy-start.9
  35.5 1.7 %copy-start.2 = (f32[6,1024,128]{2,1,0:T(8,128)}, f32[6,1024,128]{2,1,0:T(8,128)S(1)}, u32[]{:S(2)}) copy-start(f32[6,1024,128]{2,1,0:T(8,128)S(1)} %get-tuple-element.15.pre_ref) | copy-start | bytes 9437188
  37.2 1.7 %copy-start.3 = (bf16[1024,1536]{1,0:T(8,128)(2,1)}, bf16[1024,1536]{1,0:T(8,128)(2,1)S(1)}, u32[]{:S(2)}) copy-start(bf16[1024,1536]{1,0:T(8,128)(2,1)S(1)} %get-tuple-element.17.cot_ref) | copy-start | bytes 9437188
  38.9 1.1 copy-start.4
  40.1 0.8 copy-start.6
  40.9 0.8 copy-start.7
  127.9 5.6 %copy-start.10 = (f32[96,768]{1,0:T(8,128)S(1)}, f32[96,768]{1,0:T(8,128)}, u32[]{:S(2)}) copy-start(f32[96,768]{1,0:T(8,128)} %get-tuple-element.31) | copy-start | bytes 884740
Sparse Core Ops, SparseCore 0:
  10.3 44.8 all-gather.1

commit v2 on v1

--- a/solution.py
+++ b/solution.py
@@ -146,19 +146,45 @@
     return position < len_ref[u]
 
 
-def forward_kernel(
-    mp, utts, frames, taps, pad,
-    len_ref, x_ref, gain_ref, bias_ref, tap_ref, target_ref,
-    masked_ref, pre_ref, act_ref, cot_ref, mean_ref, rstd_ref,
-    stat, got, sends, recvs,
+def fused_kernel(
+    mp, stages, utts, frames, taps, pad,
+    len_ref, x_ref, gain_ref, bias_ref, tap_ref, own_weight_ref, target_ref,
+    out_ref, wgrad_ref, taps_ref, gain_out, bias_out,
+    masked_ref, pre_ref, act_ref, cot_ref, mean_ref, rstd_ref, weight_ref,
+    term, core_got, a1, a2, a3, b1, b2, b3,
+    pgrad, hat, hat_sum, hat_dot, tap_acc, stat, got, hat_stat, hat_got,
+    count, count_got, small, small_got,
+    stat_s, stat_r, all_s, all_r,
+    core_s, core_r, ring_s, ring_r, hat_s, hat_r, cnt_s, cnt_r, sm_s, sm_r, fetch_sem,
 ):
     tok, chan = x_ref.shape
     groups = tok // LANES
     blocks = chan // LANES
     span = frames + 2 * pad
-    peers = mp_peers(mp)
-    greet(peers)
+    width = cot_ref.shape[1]
+    per_utt = frames // CHUNK
+    half = chan // 2
+    out_rows = wgrad_ref.shape[0]
+    highs = term.shape[0]
+    row_peers = mp_peers(mp)
+    bits, peers = dp_bits(stages)
+    fetch = pltpu.make_async_copy(target_ref, cot_ref, fetch_sem)
+    fetch.start()
+    greet(peers + row_peers)
+    core, why, zlo, zhi = bits
     eye = eye_mask()
+    weight_ref[zhi, zlo, why, core] = own_weight_ref[...]
+    pieces = [
+        weight_ref.at[zhi, zlo, why, core],
+        weight_ref.at[:, zlo, why, core],
+        weight_ref.at[:, :, why, core],
+        weight_ref.at[:, :, :, core],
+    ]
+    gathers = [
+        rcopy(piece, piece, all_s, all_r, i, peers[stages - 1 - i])
+        for i, piece in enumerate(pieces)
+    ]
+    gathers[0].start()
 
     def stats(g, _):
         values = x_ref[rows_at(g * LANES, LANES, LANES), :].astype(F32)
@@ -171,7 +197,7 @@
 
     lax.fori_loop(0, groups, stats, 0)
     copies = [
-        rcopy(stat, got.at[s], sends, recvs, s, peer) for s, peer in enumerate(peers)
+        rcopy(stat, got.at[s], stat_s, stat_r, s, peer) for s, peer in enumerate(row_peers)
     ]
     for copy in copies:
         copy.start()
@@ -180,12 +206,13 @@
         u, part = i // (frames // CHUNK), i % (frames // CHUNK)
         rows = rows_at(i * CHUNK, CHUNK, CHUNK)
         valid = valid_rows(len_ref, u, part * CHUNK, CHUNK)
-        for c in range(target_ref.shape[1] // LANES):
+        for c in range(width // LANES):
             lanes = pl.ds(c * LANES, LANES)
-            block = target_ref[rows, lanes].astype(F32)
+            block = cot_ref[rows, lanes].astype(F32)
             cot_ref[rows, lanes] = jnp.where(valid, block, 0.0).astype(BF16)
         return 0
 
+    fetch.wait()
     lax.fori_loop(0, tok // CHUNK, mask_target, 0)
 
     def clear(i, _):
@@ -193,6 +220,8 @@
         edge = jnp.zeros((pad, LANES), F32)
         masked_ref[c, rows_at(u * span, pad, pad), :] = edge
         masked_ref[c, rows_at(u * span + pad + frames, pad, pad), :] = edge
+        pgrad[c, rows_at(u * span, pad, pad), :] = edge
+        pgrad[c, rows_at(u * span + pad + frames, pad, pad), :] = edge
         return 0
 
     lax.fori_loop(0, blocks * utts, clear, 0)
@@ -208,18 +237,21 @@
     stat[0] = mean
     stat[1] = lax.rsqrt(squares * (1.0 / (chan * mp)) + epsilon)
 
-    def spread(g, _):
+    gathers[0].wait()
+    gathers[1].start()
+
+    def spread_norm(g, _):
         rows = rows_at(g * LANES, LANES, LANES)
         shape = (LANES, LANES)
         mean_ref[rows, :] = jnp.broadcast_to(to_column(stat[0, pl.ds(g, 1), :], eye), shape)
         rstd_ref[rows, :] = jnp.broadcast_to(to_column(stat[1, pl.ds(g, 1), :], eye), shape)
         return 0
 
-    lax.fori_loop(0, groups, spread, 0)
-
-    def block(c, _):
+    lax.fori_loop(0, groups, spread_norm, 0)
+
+    def forward_block(c, _):
         lanes = lane_at(c)
-        gain, bias = gain_ref[c], bias_ref[c]
+        gain, bias = gain_ref[:, lanes], bias_ref[:, lanes]
 
         def norm(i, _):
             u, part = i // (frames // CHUNK), i % (frames // CHUNK)
@@ -246,7 +278,7 @@
                 slab = masked_ref[c, pl.ds(base + b, CHUNK + reach), :]
                 for k in ks:
                     at = (k + shift) // 8 * 8
-                    total = total + tap_ref[c, pl.ds(k, 1), :] * slab[at:at + CHUNK]
+                    total = total + tap_ref[pl.ds(k, 1), lanes] * slab[at:at + CHUNK]
             pre_ref[c, rows, :] = total
             act_ref[rows, lanes] = (total * jax.nn.sigmoid(total)).astype(BF16)
             return 0
@@ -254,32 +286,10 @@
         lax.fori_loop(0, tok // CHUNK, conv, 0)
         return 0
 
-    lax.fori_loop(0, blocks, block, 0)
-
-
-def backward_kernel(
-    mp, stages, utts, frames, taps, pad,
-    len_ref, x_ref, gain_ref, tap_ref, weight_ref,
-    masked_ref, pre_ref, act_ref, cot_ref, mean_ref, rstd_ref,
-    out_ref, wgrad_ref, small_ref,
-    term, core_got, a1, a2, a3, b1, b2, b3,
-    pgrad, hat, hat_sum, hat_dot, tap_acc, stat, got, count, count_got, small, small_got,
-    core_s, core_r, ring_s, ring_r, hat_s, hat_r, cnt_s, cnt_r, sm_s, sm_r,
-):
-    tok, chan = x_ref.shape
-    width = cot_ref.shape[1]
-    groups = tok // LANES
-    blocks = chan // LANES
-    span = frames + 2 * pad
-    per_utt = frames // CHUNK
-    half = chan // 2
-    out_rows = wgrad_ref.shape[0]
-    highs = term.shape[0]
-    row_peers = mp_peers(mp)
-    bits, peers = dp_bits(stages)
-    greet(peers + row_peers)
-    core, why, zlo, zhi = bits
-    eye = eye_mask()
+    lax.fori_loop(0, blocks // 3, forward_block, 0)
+    gathers[1].wait()
+    gathers[2].start()
+    lax.fori_loop(blocks // 3, blocks, forward_block, 0)
 
     total = len_ref[0]
     for u in range(1, utts):
@@ -292,6 +302,9 @@
     core_copies = []
     group_rows = width // highs
     for g in range(highs):
+        if g == highs - 1:
+            gathers[2].wait()
+            gathers[3].start()
         product = lax.dot_general(
             cot_ref[:, g * group_rows:(g + 1) * group_rows],
             act_ref[...],
@@ -313,18 +326,41 @@
             cnt[g + 1].start()
     inverse = 1.0 / count[stages]
 
-    def clear(i, _):
-        c, u = i // utts, i % utts
-        edge = jnp.zeros((pad, LANES), F32)
-        pgrad[c, rows_at(u * span, pad, pad), :] = edge
-        pgrad[c, rows_at(u * span + pad + frames, pad, pad), :] = edge
-        return 0
-
-    lax.fori_loop(0, blocks * utts, clear, 0)
+    for copy in core_copies:
+        copy.wait()
+
+    def join_core(i, _):
+        g, y = i // 2, i % 2
+        core_got[g, y] = core_got[g, y] + term[g, y, core]
+        return 0
+
+    lax.fori_loop(0, highs * 2, join_core, 0)
+    left, right = pl.ds(0, half), pl.ds(half, half)
+
+    copy_a1 = rcopy(core_got.at[:, 1 - why, :, left], a1, ring_s, ring_r, 0, peers[1])
+    copies_b1 = [
+        rcopy(
+            core_got.at[2 * h + 1 - zlo, :, :, right], b1.at[h], ring_s, ring_r, 1 + h, peers[2]
+        )
+        for h in range(2)
+    ]
+    copies_a2 = [
+        rcopy(a1.at[2 * h + 1 - zlo], a2.at[h], ring_s, ring_r, 3 + h, peers[2])
+        for h in range(2)
+    ]
+    copy_b2 = rcopy(b1.at[1 - zhi], b2, ring_s, ring_r, 5, peers[3])
+    copy_a3 = rcopy(a2.at[1 - zhi], a3, ring_s, ring_r, 6, peers[3])
+    copy_b3 = rcopy(b2.at[1 - why], b3, ring_s, ring_r, 7, peers[1])
+
+    copy_a1.start()
+    for copy in copies_b1:
+        copy.start()
 
     def act_grad(u, _):
         rows = rows_at(u * frames, frames, frames)
-        product = jnp.dot(cot_ref[rows, :], weight_ref[...], preferred_element_type=F32)
+        product = jnp.dot(
+            cot_ref[rows, :], weight_ref[...].reshape(width, chan), preferred_element_type=F32
+        )
         for c in range(blocks):
             pre = pre_ref[c, rows, :]
             gate = jax.nn.sigmoid(pre)
@@ -334,37 +370,8 @@
             )
         return 0
 
+    gathers[3].wait()
     lax.fori_loop(0, utts, act_grad, 0)
-
-    for copy in core_copies:
-        copy.wait()
-
-    def join_core(i, _):
-        g, y = i // 2, i % 2
-        core_got[g, y] = core_got[g, y] + term[g, y, core]
-        return 0
-
-    lax.fori_loop(0, highs * 2, join_core, 0)
-    left, right = pl.ds(0, half), pl.ds(half, half)
-
-    copy_a1 = rcopy(core_got.at[:, 1 - why, :, left], a1, ring_s, ring_r, 0, peers[1])
-    copies_b1 = [
-        rcopy(
-            core_got.at[2 * h + 1 - zlo, :, :, right], b1.at[h], ring_s, ring_r, 1 + h, peers[2]
-        )
-        for h in range(2)
-    ]
-    copies_a2 = [
-        rcopy(a1.at[2 * h + 1 - zlo], a2.at[h], ring_s, ring_r, 3 + h, peers[2])
-        for h in range(2)
-    ]
-    copy_b2 = rcopy(b1.at[1 - zhi], b2, ring_s, ring_r, 5, peers[3])
-    copy_a3 = rcopy(a2.at[1 - zhi], a3, ring_s, ring_r, 6, peers[3])
-    copy_b3 = rcopy(b2.at[1 - why], b3, ring_s, ring_r, 7, peers[1])
-
-    copy_a1.start()
-    for copy in copies_b1:
-        copy.start()
 
     def second_stage():
         copy_a1.wait()
@@ -401,7 +408,7 @@
 
     def block(c, _):
         lanes = lane_at(c)
-        gain = gain_ref[c]
+        gain = gain_ref[:, lanes]
         tap_acc[...] = jnp.zeros_like(tap_acc)
 
         def part_of(i, _):
@@ -416,7 +423,7 @@
                 slab = pgrad[c, pl.ds(base + b, CHUNK + reach), :]
                 for k in ks:
                     at = (k + shift) // 8 * 8
-                    total = total + tap_ref[c, pl.ds(taps - 1 - k, 1), :] * slab[at:at + CHUNK]
+                    total = total + tap_ref[pl.ds(taps - 1 - k, 1), lanes] * slab[at:at + CHUNK]
             for b in range(8):
                 ks = [k for k in range(taps) if (k + shift) % 8 == b]
                 reach = 8 * max((k + shift) // 8 for k in ks)
@@ -439,7 +446,7 @@
 
         lax.fori_loop(0, tok // CHUNK, part_of, 0)
         sums = jnp.sum(tap_acc[...], axis=1)
-        small[0, :, lanes] = sums
+        small[c // (blocks // 2), 0, :, lane_at(c % (blocks // 2))] = sums
         return 0
 
     def reset(i, _):
@@ -449,45 +456,61 @@
         return 0
 
     lax.fori_loop(0, tok // CHUNK, reset, 0)
-    cut = [0, blocks // 2, blocks - blocks // 6, blocks]
-    lax.fori_loop(cut[0], cut[1], block, 0)
+    sm = [
+        [
+            rcopy(
+                small.at[p, s], small_got.at[p, s], sm_s, sm_r, p * stages + s, peers[s]
+            )
+            for s in range(stages)
+        ]
+        for p in range(2)
+    ]
+
+    def advance(p, s):
+        sm[p][s].wait()
+        small[p, s + 1] = small[p, s] + small_got[p, s]
+        if s + 1 < stages:
+            sm[p][s + 1].start()
+
+    lax.fori_loop(0, blocks // 2, block, 0)
     second_stage()
-    lax.fori_loop(cut[1], cut[2], block, 0)
-    third_stage()
-    lax.fori_loop(cut[2], cut[3], block, 0)
+    sm[0][0].start()
+    left_over = blocks - blocks // 2
+    for s in range(3):
+        lax.fori_loop(
+            blocks // 2 + left_over * s // 3, blocks // 2 + left_over * (s + 1) // 3, block, 0
+        )
+        if s < 2:
+            advance(0, s)
+    sm[1][0].start()
+    advance(0, 2)
 
     def collect(g, _):
         rows = rows_at(g * LANES, LANES, LANES)
-        stat[0, pl.ds(g, 1), :] = to_row(jnp.sum(hat_sum[rows, :], axis=1, keepdims=True), eye)
-        stat[1, pl.ds(g, 1), :] = to_row(jnp.sum(hat_dot[rows, :], axis=1, keepdims=True), eye)
-        return 0
-
-    sm = [
-        rcopy(small.at[s], small_got.at[s], sm_s, sm_r, s, peers[s]) for s in range(stages)
-    ]
-    sm[0].start()
+        hat_stat[0, pl.ds(g, 1), :] = to_row(jnp.sum(hat_sum[rows, :], axis=1, keepdims=True), eye)
+        hat_stat[1, pl.ds(g, 1), :] = to_row(jnp.sum(hat_dot[rows, :], axis=1, keepdims=True), eye)
+        return 0
+
     lax.fori_loop(0, groups, collect, 0)
     hats = [
-        rcopy(stat, got.at[s], hat_s, hat_r, s, peer) for s, peer in enumerate(row_peers)
+        rcopy(hat_stat, hat_got.at[s], hat_s, hat_r, s, peer) for s, peer in enumerate(row_peers)
     ]
     for copy in hats:
         copy.start()
-    sm[0].wait()
-    small[1] = small[0] + small_got[0]
-    sm[1].start()
+    advance(1, 0)
     for copy in hats:
         copy.wait()
     for j in range(2):
-        joined = stat[j]
+        joined = hat_stat[j]
         for s in range(mp - 1):
-            joined = joined + got[s, j]
-        stat[j] = joined * (1.0 / width)
+            joined = joined + hat_got[s, j]
+        hat_stat[j] = joined * (1.0 / width)
 
     def spread(g, _):
         rows = rows_at(g * LANES, LANES, LANES)
         shape = (LANES, LANES)
-        hat_sum[rows, :] = jnp.broadcast_to(to_column(stat[0, pl.ds(g, 1), :], eye), shape)
-        hat_dot[rows, :] = jnp.broadcast_to(to_column(stat[1, pl.ds(g, 1), :], eye), shape)
+        hat_sum[rows, :] = jnp.broadcast_to(to_column(hat_stat[0, pl.ds(g, 1), :], eye), shape)
+        hat_dot[rows, :] = jnp.broadcast_to(to_column(hat_stat[1, pl.ds(g, 1), :], eye), shape)
         return 0
 
     lax.fori_loop(0, groups, spread, 0)
@@ -507,14 +530,19 @@
         return 0
 
     parts = tok // CHUNK
-    marks = [parts * s // (stages - 1) for s in range(stages)]
-    for s in range(1, stages):
-        lax.fori_loop(marks[s - 1], marks[s], finish, 0)
-        sm[s].wait()
-        small[s + 1] = small[s] + small_got[s]
-        if s + 1 < stages:
-            sm[s + 1].start()
-    small_ref[...] = small[stages] * inverse[0:1, 0:1]
+    lax.fori_loop(0, parts // 3, finish, 0)
+    advance(1, 1)
+    third_stage()
+    lax.fori_loop(parts // 3, parts * 2 // 3, finish, 0)
+    advance(0, 3)
+    advance(1, 2)
+    lax.fori_loop(parts * 2 // 3, parts, finish, 0)
+    advance(1, 3)
+    for p, part in enumerate((left, right)):
+        sums = small[p, stages] * inverse[0:1, 0:1]
+        taps_ref[:, part] = sums[:taps]
+        gain_out[part] = sums[taps]
+        bias_out[part] = sums[taps + 1]
     last_stage()
 
 
@@ -532,52 +560,33 @@
     out_rows = width // dp
     highs = dp // 4
     half = chan // 2
-    gathered = lax.all_gather(point_weight, "dp", axis=0, tiled=True)
-    gain = ln_gain.reshape(blocks, 1, LANES)
-    bias = ln_bias.reshape(blocks, 1, LANES)
-    tap_blocks = kernel.reshape(taps, blocks, LANES).transpose(1, 0, 2)
+    gain = ln_gain.reshape(1, chan)
+    bias = ln_bias.reshape(1, chan)
     vmem = pl.BlockSpec(memory_space=pltpu.VMEM)
     smem = pl.BlockSpec(memory_space=pltpu.SMEM)
     dma = pltpu.SemaphoreType.DMA
     shape = jax.ShapeDtypeStruct
     peers = max(mp - 1, 1)
-    masked, pre, act, cot, mean, rstd = pl.pallas_call(
-        functools.partial(forward_kernel, mp, utts, frames, taps, pad),
-        out_shape=(
-            shape((blocks, span, LANES), F32),
-            shape((blocks, tok, LANES), F32),
-            shape((tok, chan), BF16),
-            shape((tok, width), BF16),
-            shape((tok, LANES), F32),
-            shape((tok, LANES), F32),
-        ),
-        in_specs=[smem] + [vmem] * 5,
-        out_specs=(vmem,) * 6,
-        scratch_shapes=[
-            pltpu.VMEM((2, groups, LANES), F32),
-            pltpu.VMEM((peers, 2, groups, LANES), F32),
-            dma((peers,)),
-            dma((peers,)),
-        ],
-        compiler_params=pltpu.CompilerParams(
-            collective_id=0, has_side_effects=True, vmem_limit_bytes=40 * 2**20
-        ),
-        cost_estimate=pl.CostEstimate(
-            flops=40 * tok * chan * taps, bytes_accessed=24 * tok * chan, transcendentals=tok * chan
-        ),
-        name="forward",
-    )(lengths, frames_in, gain, bias, tap_blocks, target)
     side = (taps + 2 + 7) // 8 * 8
-    frames_grad, weight_grad, small = pl.pallas_call(
-        functools.partial(backward_kernel, mp, stages, utts, frames, taps, pad),
+    return pl.pallas_call(
+        functools.partial(fused_kernel, mp, stages, utts, frames, taps, pad),
         out_shape=(
             shape((tok, chan), BF16),
             shape((out_rows, chan), F32),
-            shape((side, chan), F32),
+            shape((taps, chan), F32),
+            shape((chan,), F32),
+            shape((chan,), F32),
         ),
-        in_specs=[smem] + [vmem] * 10,
-        out_specs=(vmem,) * 3,
+        in_specs=[smem] + [vmem] * 5 + [pl.BlockSpec(memory_space=pl.ANY)],
+        out_specs=(vmem,) * 5,
         scratch_shapes=[
+            pltpu.VMEM((blocks, span, LANES), F32),
+            pltpu.VMEM((blocks, tok, LANES), F32),
+            pltpu.VMEM((tok, chan), BF16),
+            pltpu.VMEM((tok, width), BF16),
+            pltpu.VMEM((tok, LANES), F32),
+            pltpu.VMEM((tok, LANES), F32),
+            pltpu.VMEM((2, 2, 2, 2, out_rows, chan), BF16),
             pltpu.VMEM((highs, 2, 2, out_rows, chan), F32),
             pltpu.VMEM((highs, 2, out_rows, chan), F32),
             pltpu.VMEM((highs, out_rows, half), F32),
@@ -593,10 +602,16 @@
             pltpu.VMEM((side, 8, LANES), F32),
             pltpu.VMEM((2, groups, LANES), F32),
             pltpu.VMEM((peers, 2, groups, LANES), F32),
+            pltpu.VMEM((2, groups, LANES), F32),
+            pltpu.VMEM((peers, 2, groups, LANES), F32),
             pltpu.VMEM((stages + 1, 8, LANES), F32),
             pltpu.VMEM((stages, 8, LANES), F32),
-            pltpu.VMEM((stages + 1, side, chan), F32),
-            pltpu.VMEM((stages, side, chan), F32),
+            pltpu.VMEM((2, stages + 1, side, half), F32),
+            pltpu.VMEM((2, stages, side, half), F32),
+            dma((peers,)),
+            dma((peers,)),
+            dma((stages,)),
+            dma((stages,)),
             dma((highs,)),
             dma((highs,)),
             dma((8,)),
@@ -605,15 +620,15 @@
             dma((peers,)),
             dma((stages,)),
             dma((stages,)),
-            dma((stages,)),
-            dma((stages,)),
+            dma((2 * stages,)),
+            dma((2 * stages,)),
+            dma(()),
         ],
         compiler_params=pltpu.CompilerParams(
-            collective_id=1, has_side_effects=True, vmem_limit_bytes=56 * 2**20
+            collective_id=0, has_side_effects=True, vmem_limit_bytes=56 * 2**20
         ),
-        name="backward",
-    )(lengths, frames_in, gain, tap_blocks, gathered, masked, pre, act, cot, mean, rstd)
-    return (frames_grad, weight_grad, small[:taps], small[taps], small[taps + 1])
+        name="fused",
+    )(lengths, frames_in, gain, bias, kernel, point_weight, target)
 
 
 def solution(mesh):
@@ -631,7 +646,7 @@
             and tok % LANES == 0
             and frames % CHUNK == 0
             and width % (dp // 4 * LANES) == 0
-            and width % (dp * 8) == 0
+            and width % (dp * 16) == 0
             and kernel.shape[0] % 2 == 1
             and kernel.shape[0] <= 31
         )

time: 141 us -> 98.5 us (0.70)
  waiting for transfers between devices: 14.2 us -> 0 us
  between operations: 14.1 us -> 0.68 us
  local copies, waits for them, and re-layouts: 18.8 us -> 7.79 us
  Pallas kernels: 94 us -> 89.8 us
    all_gather x1 -> x0, waiting for transfers between devices: 13.5 us -> none  [fast_body(): gathered = lax.all_gather(point_weight, 'dp', axis=0, tiled=True)]
    unnamed x24 -> x13, local copies, waits for them, and re-layouts: 13.5 us -> 5.25 us
    pallas_call x2 -> x1, Pallas kernels: 94 us -> 89.8 us  [fast_body(): pl.pallas_call(functools.partial(fused_kernel, mp, stages, utts, frames,...]
    slice x2 -> x0, local copies, waits for them, and re-layouts: 2.95 us -> none  [the longest x1 1.54 us: fast_body(): small[:taps]]
  transfers between devices with their start and end apart: 1 -> 0, of which waited for: 1 -> 0; matrix products, arithmetic and copies ran while one was open for 2% -> 0% of each run, Pallas kernels for 15% -> 0%
where the time goes in v2:
time: 98.5 us; the launch traced here: 98.3 us
  Pallas kernels  89.8 us (91%)
  local copies, waits for them, and re-layouts  7.79 us (8%)
    pallas_call x1, Pallas kernels, fast_body(): pl.pallas_call(functools.partial(fused_kernel, mp, stages, utts, frames,...  89.8 us
    unnamed x13, local copies, waits for them, and re-layouts  5.25 us

profile of v2, /device:TPU:0, one launch (start us, length us, event | category | flops | bytes accessed | tf_op | source)
XLA Modules:
  0.0 98.3 jit_solution(13738611156499989702)
XLA Ops:
  0.6 1.3 %reshape.16.gain_ref = f32[1,768]{1,0:T(1,128)} reshape(f32[768]{0:T(1024)} %param.9) | data formatting | bytes 6144 | tf_op jit(solution)/shard_map/reshape | solution.py:563
  1.9 1.3 %reshape.17.bias_ref = f32[1,768]{1,0:T(1,128)} reshape(f32[768]{0:T(1024)} %param.10) | data formatting | bytes 6144 | tf_op jit(solution)/shard_map/reshape | solution.py:564
  3.2 89.8 %fused.1 = (bf16[1024,768]{1,0:T(8,128)(2,1)}, f32[96,768]{1,0:T(8,128)}, f32[31,768]{1,0:T(8,128)}, f32[768]{0:T(1024)}, f32[768]{0:T(1024)}) custom-call(s32[4]{0:T(128)} %len_ref.1, bf16[1024,768]{1,0:T(8,128)(2,1)} %x_ref.1, f32[1,768]{1,0:T(1,128)} %reshape.16.gain_ref, f32[1,768]{1,0:T(1,128)} %reshape.17.bias_ref, f32[31,768]{1,0:T(8,128)} %tap_ref.1, ...), custom_call_target="tpu_custom_call" | custom-call | tf_op jit(solution)/shard_map/fused/pallas_call | solution.py:571
  93.0 0.0 copy-start
  93.0 0.0 copy-start.1
  93.0 0.0 copy-start.3
  93.0 0.0 copy-start.2
  93.0 2.7 %copy.17 = bf16[1024,768]{1,0:T(8,128)(2,1)} copy(bf16[1024,768]{1,0:T(8,128)(2,1)} %get-tuple-element.10) | data formatting | bytes 3145728
  95.7 0.0 copy-done
  95.7 0.7 copy.18
  96.4 0.0 copy-done.1
  96.4 0.6 copy.19
  97.1 0.0 copy-done.3
  97.1 0.6 copy.20
  97.7 0.0 copy-done.2
  97.7 0.6 copy.21
Async XLA Ops:
  93.0 2.7 %copy-start = (f32[96,768]{1,0:T(8,128)S(1)}, f32[96,768]{1,0:T(8,128)}, u32[]{:S(2)}) copy-start(f32[96,768]{1,0:T(8,128)} %get-tuple-element.11) | copy-start | bytes 884740
  93.0 3.4 %copy-start.1 = (f32[31,768]{1,0:T(8,128)S(1)}, f32[31,768]{1,0:T(8,128)}, u32[]{:S(2)}) copy-start(f32[31,768]{1,0:T(8,128)} %get-tuple-element.12) | copy-start | bytes 285700
  93.0 4.1 %copy-start.3 = (f32[768]{0:T(1024)S(1)}, f32[768]{0:T(1024)}, u32[]{:S(2)}) copy-start(f32[768]{0:T(1024)} %get-tuple-element.13) | copy-start | bytes 9220
  93.0 4.7 %copy-start.2 = (f32[768]{0:T(1024)S(1)}, f32[768]{0:T(1024)}, u32[]{:S(2)}) copy-start(f32[768]{0:T(1024)} %get-tuple-element.14) | copy-start | bytes 9220

commit v3 on v2

--- a/solution.py
+++ b/solution.py
@@ -173,18 +173,48 @@
     greet(peers + row_peers)
     core, why, zlo, zhi = bits
     eye = eye_mask()
+    left, right = pl.ds(0, half), pl.ds(half, half)
     weight_ref[zhi, zlo, why, core] = own_weight_ref[...]
-    pieces = [
-        weight_ref.at[zhi, zlo, why, core],
-        weight_ref.at[:, zlo, why, core],
-        weight_ref.at[:, :, why, core],
-        weight_ref.at[:, :, :, core],
+    gather_a = [
+        (weight_ref.at[zhi, zlo, why, core, :, left], 3),
+        (weight_ref.at[:, zlo, why, core, :, left], 2),
+        (weight_ref.at[:, :, why, core, :, left], 1),
+        (weight_ref.at[:, :, :, core, :, left], 0),
+    ]
+    gather_b = [
+        (weight_ref.at[zhi, zlo, why, core, :, right], 1),
+        (weight_ref.at[zhi, zlo, :, core, :, right], 3),
+        (weight_ref.at[:, zlo, :, core, :, right], 2),
+        (weight_ref.at[:, :, :, core, :, right], 0),
     ]
     gathers = [
-        rcopy(piece, piece, all_s, all_r, i, peers[stages - 1 - i])
-        for i, piece in enumerate(pieces)
-    ]
-    gathers[0].start()
+        [
+            rcopy(piece, piece, all_s, all_r, p * stages + i, peers[bit])
+            for i, (piece, bit) in enumerate(pieces)
+        ]
+        for p, pieces in enumerate((gather_a, gather_b))
+    ]
+
+    def gather_next(p, i):
+        gathers[p][i].wait()
+        gathers[p][i + 1].start()
+
+    gathers[0][0].start()
+    gathers[1][0].start()
+    total = len_ref[0]
+    for u in range(1, utts):
+        total = total + len_ref[u]
+    count[0] = jnp.full((8, LANES), total, jnp.int32).astype(F32)
+    cnt = [
+        rcopy(count.at[s], count_got.at[s], cnt_s, cnt_r, s, peers[s]) for s in range(stages)
+    ]
+    cnt[0].start()
+
+    def count_next(s):
+        cnt[s].wait()
+        count[s + 1] = count[s] + count_got[s]
+        if s + 1 < stages:
+            cnt[s + 1].start()
 
     def stats(g, _):
         values = x_ref[rows_at(g * LANES, LANES, LANES), :].astype(F32)
@@ -237,8 +267,8 @@
     stat[0] = mean
     stat[1] = lax.rsqrt(squares * (1.0 / (chan * mp)) + epsilon)
 
-    gathers[0].wait()
-    gathers[1].start()
+    gather_next(0, 0)
+    gather_next(1, 0)
 
     def spread_norm(g, _):
         rows = rows_at(g * LANES, LANES, LANES)
@@ -286,25 +316,20 @@
         lax.fori_loop(0, tok // CHUNK, conv, 0)
         return 0
 
-    lax.fori_loop(0, blocks // 3, forward_block, 0)
-    gathers[1].wait()
-    gathers[2].start()
-    lax.fori_loop(blocks // 3, blocks, forward_block, 0)
-
-    total = len_ref[0]
-    for u in range(1, utts):
-        total = total + len_ref[u]
-    count[0] = jnp.full((8, LANES), total, jnp.int32).astype(F32)
-    cnt = [
-        rcopy(count.at[s], count_got.at[s], cnt_s, cnt_r, s, peers[s]) for s in range(stages)
-    ]
-    cnt[0].start()
+    for s in range(6):
+        lax.fori_loop(blocks * s // 6, blocks * (s + 1) // 6, forward_block, 0)
+        if s < stages:
+            count_next(s)
+        if s == 1:
+            gather_next(0, 1)
+            gather_next(1, 1)
+        if s == 4:
+            gather_next(0, 2)
+            gather_next(1, 2)
+
     core_copies = []
     group_rows = width // highs
     for g in range(highs):
-        if g == highs - 1:
-            gathers[2].wait()
-            gathers[3].start()
         product = lax.dot_general(
             cot_ref[:, g * group_rows:(g + 1) * group_rows],
             act_ref[...],
@@ -320,10 +345,6 @@
         )
         copy.start()
         core_copies.append(copy)
-        cnt[g].wait()
-        count[g + 1] = count[g] + count_got[g]
-        if g + 1 < stages:
-            cnt[g + 1].start()
     inverse = 1.0 / count[stages]
 
     for copy in core_copies:
@@ -335,7 +356,6 @@
         return 0
 
     lax.fori_loop(0, highs * 2, join_core, 0)
-    left, right = pl.ds(0, half), pl.ds(half, half)
 
     copy_a1 = rcopy(core_got.at[:, 1 - why, :, left], a1, ring_s, ring_r, 0, peers[1])
     copies_b1 = [
@@ -370,7 +390,8 @@
             )
         return 0
 
-    gathers[3].wait()
+    gathers[0][3].wait()
+    gathers[1][3].wait()
     lax.fori_loop(0, utts, act_grad, 0)
 
     def second_stage():
@@ -500,6 +521,7 @@
     advance(1, 0)
     for copy in hats:
         copy.wait()
+    third_stage()
     for j in range(2):
         joined = hat_stat[j]
         for s in range(mp - 1):
@@ -532,7 +554,6 @@
     parts = tok // CHUNK
     lax.fori_loop(0, parts // 3, finish, 0)
     advance(1, 1)
-    third_stage()
     lax.fori_loop(parts // 3, parts * 2 // 3, finish, 0)
     advance(0, 3)
     advance(1, 2)
@@ -610,8 +631,8 @@
             pltpu.VMEM((2, stages, side, half), F32),
             dma((peers,)),
             dma((peers,)),
-            dma((stages,)),
-            dma((stages,)),
+            dma((2 * stages,)),
+            dma((2 * stages,)),
             dma((highs,)),
             dma((highs,)),
             dma((8,)),

time: 98.5 us -> 91.3 us (0.927)
  Pallas kernels: 89.8 us -> 82.6 us
    pallas_call x1, Pallas kernels: 89.8 us -> 82.6 us  [fast_body(): pl.pallas_call(functools.partial(fused_kernel, mp, stages, utts, frames,...]
where the time goes in v3:
time: 91.3 us; the launch traced here: 91.1 us
  Pallas kernels  82.6 us (90%)
  local copies, waits for them, and re-layouts  7.79 us (9%)
    pallas_call x1, Pallas kernels, fast_body(): pl.pallas_call(functools.partial(fused_kernel, mp, stages, utts, frames,...  82.6 us
    unnamed x13, local copies, waits for them, and re-layouts  5.25 us

profile of v3, /device:TPU:0, one launch (start us, length us, event | category | flops | bytes accessed | tf_op | source)
XLA Modules:
  0.0 91.1 jit_solution(2181943485360023495)
XLA Ops:
  0.6 1.3 %reshape.16.gain_ref = f32[1,768]{1,0:T(1,128)} reshape(f32[768]{0:T(1024)} %param.9) | data formatting | bytes 6144 | tf_op jit(solution)/shard_map/reshape | solution.py:584
  1.9 1.3 %reshape.17.bias_ref = f32[1,768]{1,0:T(1,128)} reshape(f32[768]{0:T(1024)} %param.10) | data formatting | bytes 6144 | tf_op jit(solution)/shard_map/reshape | solution.py:585
  3.2 82.6 %fused.1 = (bf16[1024,768]{1,0:T(8,128)(2,1)}, f32[96,768]{1,0:T(8,128)}, f32[31,768]{1,0:T(8,128)}, f32[768]{0:T(1024)}, f32[768]{0:T(1024)}) custom-call(s32[4]{0:T(128)} %len_ref.1, bf16[1024,768]{1,0:T(8,128)(2,1)} %x_ref.1, f32[1,768]{1,0:T(1,128)} %reshape.16.gain_ref, f32[1,768]{1,0:T(1,128)} %reshape.17.bias_ref, f32[31,768]{1,0:T(8,128)} %tap_ref.1, ...), custom_call_target="tpu_custom_call" | custom-call | tf_op jit(solution)/shard_map/fused/pallas_call | solution.py:592
  85.8 0.0 copy-start
  85.8 0.0 copy-start.1
  85.8 0.0 copy-start.3
  85.8 0.0 copy-start.2
  85.8 2.7 %copy.17 = bf16[1024,768]{1,0:T(8,128)(2,1)} copy(bf16[1024,768]{1,0:T(8,128)(2,1)} %get-tuple-element.10) | data formatting | bytes 3145728
  88.5 0.0 copy-done
  88.5 0.7 copy.18
  89.2 0.0 copy-done.1
  89.2 0.6 copy.19
  89.9 0.0 copy-done.3
  89.9 0.6 copy.20
  90.5 0.0 copy-done.2
  90.5 0.6 copy.21
Async XLA Ops:
  85.8 2.7 %copy-start = (f32[96,768]{1,0:T(8,128)S(1)}, f32[96,768]{1,0:T(8,128)}, u32[]{:S(2)}) copy-start(f32[96,768]{1,0:T(8,128)} %get-tuple-element.11) | copy-start | bytes 884740
  85.8 3.4 %copy-start.1 = (f32[31,768]{1,0:T(8,128)S(1)}, f32[31,768]{1,0:T(8,128)}, u32[]{:S(2)}) copy-start(f32[31,768]{1,0:T(8,128)} %get-tuple-element.12) | copy-start | bytes 285700
  85.8 4.1 %copy-start.3 = (f32[768]{0:T(1024)S(1)}, f32[768]{0:T(1024)}, u32[]{:S(2)}) copy-start(f32[768]{0:T(1024)} %get-tuple-element.13) | copy-start | bytes 9220
  85.8 4.7 %copy-start.2 = (f32[768]{0:T(1024)S(1)}, f32[768]{0:T(1024)}, u32[]{:S(2)}) copy-start(f32[768]{0:T(1024)} %get-tuple-element.14) | copy-start | bytes 9220

commit v4 on v3

--- a/solution.py
+++ b/solution.py
@@ -148,9 +148,9 @@
 
 def fused_kernel(
     mp, stages, utts, frames, taps, pad,
-    len_ref, x_ref, gain_ref, bias_ref, tap_ref, own_weight_ref, target_ref,
+    len_ref, x_ref, gain_in, bias_in, tap_ref, own_weight_ref, target_ref,
     out_ref, wgrad_ref, taps_ref, gain_out, bias_out,
-    masked_ref, pre_ref, act_ref, cot_ref, mean_ref, rstd_ref, weight_ref,
+    gain_ref, bias_ref, masked_ref, pre_ref, act_ref, cot_ref, mean_ref, rstd_ref, weight_ref,
     term, core_got, a1, a2, a3, b1, b2, b3,
     pgrad, hat, hat_sum, hat_dot, tap_acc, stat, got, hat_stat, hat_got,
     count, count_got, small, small_got,
@@ -170,6 +170,8 @@
     bits, peers = dp_bits(stages)
     fetch = pltpu.make_async_copy(target_ref, cot_ref, fetch_sem)
     fetch.start()
+    gain_ref[...] = gain_in[...].reshape(1, chan)
+    bias_ref[...] = bias_in[...].reshape(1, chan)
     greet(peers + row_peers)
     core, why, zlo, zhi = bits
     eye = eye_mask()
@@ -326,6 +328,32 @@
         if s == 4:
             gather_next(0, 2)
             gather_next(1, 2)
+
+    copies_a1 = [
+        rcopy(core_got.at[g, 1 - why, :, left], a1.at[g], ring_s, ring_r, g, peers[1])
+        for g in range(highs)
+    ]
+    copies_b1 = [
+        rcopy(
+            core_got.at[2 * h + 1 - zlo, :, :, right], b1.at[h], ring_s, ring_r, 4 + h, peers[2]
+        )
+        for h in range(2)
+    ]
+    copies_a2 = [
+        rcopy(a1.at[2 * h + 1 - zlo], a2.at[h], ring_s, ring_r, 6 + h, peers[2])
+        for h in range(2)
+    ]
+    copy_b2 = rcopy(b1.at[1 - zhi], b2, ring_s, ring_r, 8, peers[3])
+    copy_a3 = rcopy(a2.at[1 - zhi], a3, ring_s, ring_r, 9, peers[3])
+    copy_b3 = rcopy(b2.at[1 - why], b3, ring_s, ring_r, 10, peers[1])
+
+    def join_core(g):
+        core_copies[g].wait()
+        for y in range(2):
+            core_got[g, y] = core_got[g, y] + term[g, y, core]
+        copies_a1[g].start()
+        if g % 2 == 1:
+            copies_b1[g // 2].start()
 
     core_copies = []
     group_rows = width // highs
@@ -345,36 +373,11 @@
         )
         copy.start()
         core_copies.append(copy)
+        if g > 0:
+            join_core(g - 1)
     inverse = 1.0 / count[stages]
 
-    for copy in core_copies:
-        copy.wait()
-
-    def join_core(i, _):
-        g, y = i // 2, i % 2
-        core_got[g, y] = core_got[g, y] + term[g, y, core]
-        return 0
-
-    lax.fori_loop(0, highs * 2, join_core, 0)
-
-    copy_a1 = rcopy(core_got.at[:, 1 - why, :, left], a1, ring_s, ring_r, 0, peers[1])
-    copies_b1 = [
-        rcopy(
-            core_got.at[2 * h + 1 - zlo, :, :, right], b1.at[h], ring_s, ring_r, 1 + h, peers[2]
-        )
-        for h in range(2)
-    ]
-    copies_a2 = [
-        rcopy(a1.at[2 * h + 1 - zlo], a2.at[h], ring_s, ring_r, 3 + h, peers[2])
-        for h in range(2)
-    ]
-    copy_b2 = rcopy(b1.at[1 - zhi], b2, ring_s, ring_r, 5, peers[3])
-    copy_a3 = rcopy(a2.at[1 - zhi], a3, ring_s, ring_r, 6, peers[3])
-    copy_b3 = rcopy(b2.at[1 - why], b3, ring_s, ring_r, 7, peers[1])
-
-    copy_a1.start()
-    for copy in copies_b1:
-        copy.start()
+    join_core(highs - 1)
 
     def act_grad(u, _):
         rows = rows_at(u * frames, frames, frames)
@@ -395,7 +398,8 @@
     lax.fori_loop(0, utts, act_grad, 0)
 
     def second_stage():
-        copy_a1.wait()
+        for copy in copies_a1:
+            copy.wait()
         for h in range(highs):
             a1[h] = a1[h] + core_got[h, why, :, left]
         for copy in copies_a2:
@@ -581,8 +585,6 @@
     out_rows = width // dp
     highs = dp // 4
     half = chan // 2
-    gain = ln_gain.reshape(1, chan)
-    bias = ln_bias.reshape(1, chan)
     vmem = pl.BlockSpec(memory_space=pltpu.VMEM)
     smem = pl.BlockSpec(memory_space=pltpu.SMEM)
     dma = pltpu.SemaphoreType.DMA
@@ -601,6 +603,8 @@
         in_specs=[smem] + [vmem] * 5 + [pl.BlockSpec(memory_space=pl.ANY)],
         out_specs=(vmem,) * 5,
         scratch_shapes=[
+            pltpu.VMEM((1, chan), F32),
+            pltpu.VMEM((1, chan), F32),
             pltpu.VMEM((blocks, span, LANES), F32),
             pltpu.VMEM((blocks, tok, LANES), F32),
             pltpu.VMEM((tok, chan), BF16),
@@ -635,8 +639,8 @@
             dma((2 * stages,)),
             dma((highs,)),
             dma((highs,)),
-            dma((8,)),
-            dma((8,)),
+            dma((11,)),
+            dma((11,)),
             dma((peers,)),
             dma((peers,)),
             dma((stages,)),
@@ -649,7 +653,7 @@
             collective_id=0, has_side_effects=True, vmem_limit_bytes=56 * 2**20
         ),
         name="fused",
-    )(lengths, frames_in, gain, bias, kernel, point_weight, target)
+    )(lengths, frames_in, ln_gain, ln_bias, kernel, point_weight, target)
 
 
 def solution(mesh):

time: 91.3 us -> 86.4 us (0.946)
  local copies, waits for them, and re-layouts: 7.79 us -> 5.25 us
  Pallas kernels: 82.6 us -> 80.3 us
    reshape x2 -> x0, local copies, waits for them, and re-layouts: 2.53 us -> none  [the longest x1 1.27 us: fast_body(): gain = ln_gain.reshape(1, chan)]
    pallas_call x1, Pallas kernels: 82.6 us -> 80.3 us  [fast_body(): pl.pallas_call(functools.partial(fused_kernel, mp, stages, utts, frames,...]
where the time goes in v4:
time: 86.4 us; the launch traced here: 86.2 us
  Pallas kernels  80.3 us (93%)
  local copies, waits for them, and re-layouts  5.25 us (6%)
    pallas_call x1, Pallas kernels, fast_body(): pl.pallas_call(functools.partial(fused_kernel, mp, stages, utts, frames,...  80.3 us
    unnamed x13, local copies, waits for them, and re-layouts  5.25 us

profile of v4, /device:TPU:0, one launch (start us, length us, event | category | flops | bytes accessed | tf_op | source)
XLA Modules:
  0.0 86.2 jit_solution(1573194486021755413)
XLA Ops:
  0.6 80.3 %fused.1 = (bf16[1024,768]{1,0:T(8,128)(2,1)}, f32[96,768]{1,0:T(8,128)}, f32[31,768]{1,0:T(8,128)}, f32[768]{0:T(1024)}, f32[768]{0:T(1024)}) custom-call(s32[4]{0:T(128)} %len_ref.1, bf16[1024,768]{1,0:T(8,128)(2,1)} %x_ref.1, f32[768]{0:T(1024)} %gain_in.1, f32[768]{0:T(1024)} %bias_in.1, f32[31,768]{1,0:T(8,128)} %tap_ref.1, ...), custom_call_target="tpu_custom_call" | custom-call | tf_op jit(solution)/shard_map/fused/pallas_call | solution.py:594
  81.0 0.0 copy-start
  81.0 0.0 copy-start.1
  81.0 0.0 copy-start.3
  81.0 0.0 copy-start.2
  81.0 2.7 %copy.17 = bf16[1024,768]{1,0:T(8,128)(2,1)} copy(bf16[1024,768]{1,0:T(8,128)(2,1)} %get-tuple-element.10) | data formatting | bytes 3145728
  83.7 0.0 copy-done
  83.7 0.7 copy.18
  84.4 0.0 copy-done.1
  84.4 0.6 copy.19
  85.1 0.0 copy-done.3
  85.1 0.6 copy.20
  85.7 0.0 copy-done.2
  85.7 0.6 copy.21
Async XLA Ops:
  81.0 2.7 %copy-start = (f32[96,768]{1,0:T(8,128)S(1)}, f32[96,768]{1,0:T(8,128)}, u32[]{:S(2)}) copy-start(f32[96,768]{1,0:T(8,128)} %get-tuple-element.11) | copy-start | bytes 884740
  81.0 3.4 %copy-start.1 = (f32[31,768]{1,0:T(8,128)S(1)}, f32[31,768]{1,0:T(8,128)}, u32[]{:S(2)}) copy-start(f32[31,768]{1,0:T(8,128)} %get-tuple-element.12) | copy-start | bytes 285700
  81.0 4.1 %copy-start.3 = (f32[768]{0:T(1024)S(1)}, f32[768]{0:T(1024)}, u32[]{:S(2)}) copy-start(f32[768]{0:T(1024)} %get-tuple-element.13) | copy-start | bytes 9220
  81.0 4.7 %copy-start.2 = (f32[768]{0:T(1024)S(1)}, f32[768]{0:T(1024)}, u32[]{:S(2)}) copy-start(f32[768]{0:T(1024)} %get-tuple-element.14) | copy-start | bytes 9220
